TPU v7x, 128 devices: a whole 4x4x4 slice. The times are simulated.
128 devices in a mesh: grp: 4 (over z), inner: 32 (over y, x, core).
Axes of the slice: x: 4, y: 4, z: 4, core: 2. Of those that a mesh axis runs over, the one named last changes fastest.
Arguments:
- averaged_features: bfloat16 [131072, 1152], P(('grp', 'inner')), may hold values from -6 to 6
- caption_embeddings_raw: bfloat16 [131072, 1152], P(('grp', 'inner')), may hold values from -6 to 6
- mapping_matrix: bfloat16 [1152, 1152], replicated, may hold values from -0.1875 to 0.1875
- logit_scaling: float32 [1], replicated, may hold values from 5 to 15
- logit_offset: float32 [1], replicated, may hold values from -3 to -1
- partner_picture_segment: int32 [4, 32, 4, 2], P(None, 'inner'), may hold values from 0 to 1
- partner_caption_segment: int32 [4, 32, 4, 2], P(None, 'inner'), may hold values from 0 to 1, as said below
- active_partner_total: int32 [4, 32, 4], P(None, 'inner'), may hold values from 0 to 2, as said below
Outputs:
- row_loss: float32 [131072], P(('grp', 'inner'))
- d_pooled: bfloat16 [131072, 1152], P(('grp', 'inner'))
- d_text: bfloat16 [131072, 1152], P(('grp', 'inner'))
- d_head: float32 [1152, 1152], P('inner')
Inputs may be any that keep to these rules, and one draw needn't show every extreme that they name: `partner_caption_segment`: the 2 text blocks of one (g, i, h) are distinct. active_partner_total[g, i, g] is 0; the value 2 is taken in every draw.
All inputs are finite; a program needn't handle non-finite values.
Results may differ from a plain program's by a relative error of at most 0.023.
Values may be sent and summed in bfloat16 or wider, within the bound.
A program may use at most 192 MiB of HBM per device.

v0:
```python
import jax
import jax.numpy as jnp
from jax import lax
from jax.sharding import PartitionSpec as P

BLK = 512
PER_GRP = 2


NORM_EPSILON = 1e-06


def unit_rows(values):
    reciprocal_norm = lax.rsqrt(jnp.sum(values * values, axis=-1, keepdims=True) + NORM_EPSILON)
    return (values * reciprocal_norm, reciprocal_norm)


def patch_contributions(
    picture_segment, caption_segment, scaling_scalar, offset_scalar, matching_term, active_filter
):
    similarity_scores_raw = (
        scaling_scalar
        * jnp.dot(picture_segment, caption_segment.T, preferred_element_type=jnp.float32)
        + offset_scalar
    )
    label_sign = 2.0 * matching_term - 1.0
    line_contributions = (
        jnp.sum(jax.nn.softplus(-label_sign * similarity_scores_raw), axis=1) * active_filter
    )
    derivative_patch = (
        -label_sign * jax.nn.sigmoid(-label_sign * similarity_scores_raw) * active_filter
    ).astype(jnp.bfloat16)
    picture_derivative = scaling_scalar * jnp.dot(
        derivative_patch, caption_segment, preferred_element_type=jnp.float32
    )
    caption_derivative = scaling_scalar * jnp.dot(
        derivative_patch.T, picture_segment, preferred_element_type=jnp.float32
    )
    return (line_contributions, picture_derivative, caption_derivative)


def project_back(grad_unit, unit32, reciprocal_norm):
    along = jnp.sum(grad_unit * unit32, axis=-1, keepdims=True)
    return (grad_unit - unit32 * along) * reciprocal_norm


def per_device(
    averaged_features,
    caption_embeddings_raw,
    mapping_matrix,
    logit_scaling,
    logit_offset,
    partner_picture_segment,
    partner_caption_segment,
    active_partner_total,
):
    groups = lax.axis_size("grp")
    my_group = lax.axis_index("grp")
    width = averaged_features.shape[1]
    blocks = averaged_features.shape[0] // BLK
    slots = groups * PER_GRP
    embedded = jnp.dot(averaged_features, mapping_matrix, preferred_element_type=jnp.float32)
    image_unit32, image_inv = unit_rows(embedded)
    text_unit32, text_inv = unit_rows(caption_embeddings_raw.astype(jnp.float32))
    picture_segments = image_unit32.astype(jnp.bfloat16).reshape(blocks, BLK, width)
    caption_segments = text_unit32.astype(jnp.bfloat16).reshape(blocks, BLK, width)
    scaling_scalar = logit_scaling[0]
    offset_scalar = logit_offset[0]
    diag_tiles = jax.vmap(patch_contributions, in_axes=(0, 0, None, None, None, None))
    hard_tiles = jax.vmap(patch_contributions, in_axes=(0, 0, None, None, None, 0))
    row_sums, image_grads, text_grads = diag_tiles(
        picture_segments,
        caption_segments,
        scaling_scalar,
        offset_scalar,
        jnp.eye(BLK, dtype=jnp.float32),
        1.0,
    )
    my_image = lax.dynamic_index_in_dim(partner_picture_segment[:, 0], my_group, 0, keepdims=False)
    my_text = lax.dynamic_index_in_dim(partner_caption_segment[:, 0], my_group, 0, keepdims=False)
    my_count = lax.dynamic_index_in_dim(active_partner_total[:, 0], my_group, 0, keepdims=False)
    slot_index = jnp.arange(PER_GRP, dtype=jnp.int32)
    local_active = (slot_index[None, :] < my_count[:, None]).astype(jnp.float32).reshape(slots)
    picture_position = my_image.reshape(slots)
    selected_pictures = picture_segments[picture_position]
    mismatched_term = jnp.zeros((BLK, BLK), jnp.float32)
    collected_entries = lax.all_gather(caption_segments, "grp", axis=0, tiled=True)
    caption_position = (jnp.arange(groups, dtype=jnp.int32)[:, None] * blocks + my_text).reshape(
        slots
    )
    hard_rows, hard_image, hard_text = hard_tiles(
        selected_pictures,
        collected_entries[caption_position],
        scaling_scalar,
        offset_scalar,
        mismatched_term,
        local_active,
    )
    partial_value = (
        jnp.zeros((groups * blocks, BLK, width), jnp.bfloat16)
        .at[caption_position]
        .add(hard_text.astype(jnp.bfloat16))
    )
    summed = lax.psum_scatter(
        partial_value.reshape(groups * blocks * BLK, width), "grp", scatter_dimension=0, tiled=True
    ).astype(jnp.float32)
    remote_text = summed.reshape(blocks, BLK, width)
    row_sums = row_sums.at[picture_position].add(hard_rows)
    image_grads = image_grads.at[picture_position].add(hard_image)
    text_grads = text_grads + remote_text
    embed_grad = project_back(
        image_grads.reshape(blocks * BLK, width), image_unit32, image_inv
    ).astype(jnp.bfloat16)
    d_pooled = lax.dot_general(
        embed_grad, mapping_matrix, (((1,), (1,)), ((), ())), preferred_element_type=jnp.float32
    ).astype(jnp.bfloat16)
    d_text = project_back(text_grads.reshape(blocks * BLK, width), text_unit32, text_inv).astype(
        jnp.bfloat16
    )
    column_sum = lax.psum_scatter(
        lax.dot_general(
            averaged_features,
            embed_grad,
            (((0,), (0,)), ((), ())),
            preferred_element_type=jnp.float32,
        ).astype(jnp.bfloat16),
        "inner",
        scatter_dimension=0,
        tiled=True,
    )
    d_head = lax.psum(column_sum, "grp").astype(jnp.float32)
    row_loss = row_sums.reshape(blocks * BLK) / BLK
    return (row_loss, d_pooled, d_text, d_head)


def solution(mesh):
    return jax.shard_map(
        per_device,
        mesh=mesh,
        in_specs=(
            P(("grp", "inner"), None),
            P(("grp", "inner"), None),
            P(),
            P(),
            P(),
            P(None, "inner", None, None),
            P(None, "inner", None, None),
            P(None, "inner", None),
        ),
        out_specs=(
            P(("grp", "inner")),
            P(("grp", "inner"), None),
            P(("grp", "inner"), None),
            P("inner", None),
        ),
        check_vma=False,
    )
```

profile of v0, /device:TPU:0, one launch (start us, length us, event | category | flops | bytes accessed | tf_op | source)
XLA Modules:
  0.0 455.0 jit_solution(10897941164297706969)
XLA Ops:
  7.2 2.3 fusion.10
  9.6 3.5 fusion.4
  13.2 0.7 constant_dynamic-slice_fusion.2
  13.9 0.1 copy.22
  14.0 0.1 reshape.163
  14.1 0.7 constant_dynamic-slice_fusion.1
  14.7 0.1 copy.23
  14.8 0.1 squeeze.18
  14.9 0.1 add.117
  15.0 0.1 add.118
  16.4 0.7 fusion.20
  17.0 0.1 fusion.19
  17.1 0.1 reshape.169
  17.2 5.3 %multiply_reduce_fusion = (f32[1024]{0:T(1024)S(1)}, f32[1024,1152]{1,0:T(8,128)S(1)}) fusion(bf16[1024,1152]{1,0:T(8,128)(2,1)} %param.8, bf16[1152,1152]{1,0:T(8,128)(2,1)S(1)} %copy-done), kind=kOutput, calls=%fused_computation.33 | convolution fusion | flops 2720267264 | bytes 9736192 | tf_op jit(solution)/shard_map/dot_general | solution.py:62
  22.6 2.1 copy-done.2
  24.7 1.7 multiply_convert_fusion.1
  26.4 7.5 %gather_fusion = bf16[8,512,1152]{2,1,0:T(8,128)(2,1)} fusion(bf16[2,512,1152]{2,1,0:T(8,128)(2,1)} %bitcast.60, s32[1024]{0:T(1024)S(1)} %pad_clamp_fusion.1), kind=kCustom, calls=%fused_computation | custom fusion | bytes 18874400 | tf_op jit(solution)/shard_map/gather | solution.py:85
  33.9 0.1 add_negate_fusion
  34.1 4.6 %fusion.15 = (u8[512,512]{0,1:T(8,128)(4,1)S(1)}, f32[2,512,512]{1,2,0:T(8,128)S(1)}) fusion(f32[]{:T(128)} %bitcast.54, bf16[2,512,1152]{2,1,0:T(8,128)(2,1)} %bitcast.61, bf16[2,512,1152]{2,1,0:T(8,128)(2,1)} %bitcast.64, f32[]{:T(128)} %bitcast.47, f32[512,512]{0,1:T(8,128)S(1)} %add_negate_fusion), kind=kOutput, calls=%fused_computation.44 | convolution fusion | flops 1211891712 | bytes 8126472 | tf_op jit(solution)/shard_map/vmap()/dot_general | solution.py:23
  38.7 1.3 copy-done.7
  40.0 3.8 convolution_multiply_fusion.3
  43.8 64.0 %all-gather.2.cloned.1.call-done = bf16[8,512,1152]{2,1,0:T(8,128)(2,1)} async-done(((bf16[2,512,1152]{2,1,0:T(8,128)(2,1)}), bf16[8,512,1152]{2,1,0:T(8,128)(2,1)}) %all-gather.2.cloned.1.call-update) | async-done | bytes 9437200 | tf_op jit(solution)/shard_map/all_gather | solution.py:87
  107.8 9.0 %gather_fusion.1 = bf16[8,512,1152]{2,1,0:T(8,128)(2,1)} fusion(bf16[8,512,1152]{2,1,0:T(8,128)(2,1)} %all-gather.2.cloned.1.call-done, s32[1024]{0:T(1024)S(1)} %pad_clamp_fusion), kind=kCustom, calls=%fused_computation.1 | custom fusion | bytes 18874400 | tf_op jit(solution)/shard_map/gather | solution.py:93
  116.8 14.5 %fusion.14 = (u8[512,512]{0,1:T(8,128)(4,1)S(1)}, f32[8,512,512]{1,2,0:T(8,128)}) fusion(f32[]{:T(128)} %bitcast.55, f32[]{:T(128)} %bitcast.48, bf16[8,512,1152]{2,1,0:T(8,128)(2,1)} %gather_fusion, bf16[8,512,1152]{2,1,0:T(8,128)(2,1)} %gather_fusion.1), kind=kOutput, calls=%fused_computation.41 | convolution fusion | flops 4846256128 | bytes 27525128 | tf_op jit(solution)/shard_map/vmap()/dot_general | solution.py:23
  131.4 15.3 %convolution_multiply_fusion.1 = f32[8,512,1152]{2,1,0:T(8,128)} fusion(bf16[8,512,1152]{2,1,0:T(8,128)(2,1)S(1)} %copy-done.5, f32[]{:T(128)} %bitcast.50, f32[8,512,512]{1,2,0:T(8,128)} %get-tuple-element.21, f32[8]{0:T(128)S(1)} %reshape.169, f32[]{:T(128)} %bitcast.57), kind=kOutput, calls=%fused_computation.6 | convolution fusion | flops 4851236864 | bytes 36700200 | tf_op jit(solution)/shard_map/vmap()/dot_general | solution.py:33
  146.7 32.7 %scatter_fusion = f32[2,512,1152]{2,1,0:T(8,128)} fusion(f32[2,512,1152]{2,1,0:T(8,128)} %convolution_multiply_fusion.3, s32[8]{0:T(128)S(1)} %get-tuple-element.22, f32[8,512,1152]{2,1,0:T(8,128)} %convolution_multiply_fusion.1), kind=kCustom, calls=%fused_computation.3 | custom fusion | flops 4718592 | bytes 56623136 | tf_op jit(solution)/shard_map/scatter-add | solution.py:109
  179.4 4.5 fusion.11
  183.9 0.6 copy-done.1
  184.5 3.8 fusion.13
  188.3 1.4 copy-done.6
  189.7 4.8 %fusion.1 = bf16[1152,1152]{0,1:T(8,128)(2,1)} fusion(bf16[1024,1152]{1,0:T(8,128)(2,1)S(1)} %fusion.13, bf16[1024,1152]{1,0:T(8,128)(2,1)S(1)} %copy-done.9), kind=kOutput, calls=%fused_computation.14 | convolution fusion | flops 2719236096 | bytes 7372800 | tf_op jit(solution)/shard_map/dot_general | solution.py:121
  194.6 0.0 all-reduce.4.cloned.1.call-start
  194.7 0.6 dynamic-slice.3
  195.9 107.7 %all-reduce.6.cloned.1.call-done = bf16[1152,1152]{0,1:T(8,128)(2,1)} async-done(((bf16[1152,1152]{0,1:T(8,128)(2,1)}), bf16[1152,1152]{0,1:T(8,128)(2,1)}) %all-reduce.6.cloned.1.call-update) | async-done | bytes 2654224
  303.6 1.9 constant_dynamic-slice_fusion.3
  305.6 13.1 %fusion = bf16[8,512,1152]{2,1,0:T(8,128)(2,1)} fusion(bf16[8,512,1152]{2,1,0:T(8,128)(2,1)} %gather_fusion, f32[]{:T(128)} %bitcast.51, f32[8,512,512]{1,2,0:T(8,128)} %get-tuple-element.21, f32[8]{0:T(128)S(1)} %reshape.169, f32[]{:T(128)} %bitcast.58), kind=kOutput, calls=%fused_computation.7 | convolution fusion | flops 4855955456 | bytes 27263016 | tf_op jit(solution)/shard_map/vmap()/dot_general | solution.py:36
  318.7 4.9 %broadcast_in_dim.2 = bf16[8,512,1152]{2,1,0:T(8,128)(2,1)} broadcast(bf16[]{:T(256)} %constant.48.clone.1), dimensions={} | broadcast | bytes 9437186 | tf_op jit(solution)/shard_map/broadcast_in_dim | solution.py:100
  323.5 24.3 %scatter_fusion.1 = bf16[8,512,1152]{2,1,0:T(8,128)(2,1)} fusion(bf16[8,512,1152]{2,1,0:T(8,128)(2,1)} %broadcast_in_dim.2, s32[8]{0:T(128)S(1)} %get-tuple-element.23, bf16[8,512,1152]{2,1,0:T(8,128)(2,1)} %fusion), kind=kCustom, calls=%fused_computation.4 | custom fusion | flops 4718592 | bytes 28311584 | tf_op jit(solution)/shard_map/scatter-add | solution.py:102
  347.9 2.9 select_reduce_fusion.1
  350.8 7.7 %select_reduce_fusion = f32[8,512]{1,0:T(8,128)S(1)} fusion(f32[8,512,512]{1,2,0:T(8,128)} %get-tuple-element.21, f32[]{:T(128)} %bitcast.56, f32[]{:T(128)} %bitcast.52, u8[512,512]{0,1:T(8,128)(4,1)S(1)} %get-tuple-element.20), kind=kLoop, calls=%fused_computation.11 | loop fusion | flops 25161728 | bytes 8667144 | tf_op jit(solution)/shard_map/vmap()/reduce_sum | solution.py:28
  358.5 1.0 scatter_custom_fusion
  359.5 0.6 copy.31
  360.1 6.8 %convolution_convert_fusion.1 = bf16[1024,1152]{1,0:T(8,128)(2,1)} fusion(bf16[1024,1152]{1,0:T(8,128)(2,1)} %copy-done.6, bf16[1152,1152]{1,0:T(8,128)(2,1)S(1)} %copy-done), kind=kOutput, calls=%fused_computation.35 | convolution fusion | flops 2719088640 | bytes 7372800 | tf_op jit(solution)/shard_map/dot_general | solution.py:114
  366.9 1.8 copy.26
  368.7 71.5 %reduce-scatter.3.cloned.1.call-done = bf16[1024,1152]{1,0:T(8,128)(2,1)} async-done(((bf16[4096,1152]{1,0:T(8,128)(2,1)}), bf16[1024,1152]{1,0:T(8,128)(2,1)}) %reduce-scatter.3.cloned.1.call-update) | async-done | bytes 2359312 | tf_op jit(solution)/shard_map/reduce_scatter | solution.py:104
  440.2 5.2 %fusion.5 = f32[2,512,1152]{2,1,0:T(8,128)S(1)} fusion(bf16[2,512,1152]{2,1,0:T(8,128)(2,1)} %bitcast.62, bf16[2,512,1152]{2,1,0:T(8,128)(2,1)} %bitcast.67, f32[]{:T(128)} %bitcast.53, f32[2,512,512]{1,2,0:T(8,128)} %copy-done.7, f32[512,512]{0,1:T(8,128)} %copy-done.8), kind=kOutput, calls=%fused_computation.22 | convolution fusion | flops 1214119936 | bytes 12582916 | tf_op jit(solution)/shard_map/vmap()/dot_general | solution.py:36
  445.4 0.8 fusion.6
  446.2 2.3 fusion.9
  (33 shorter events, 0.3 us)
Async XLA Ops:
  7.2 10.1 %copy-start = (bf16[1152,1152]{1,0:T(8,128)(2,1)S(1)}, bf16[1152,1152]{1,0:T(8,128)(2,1)}, u32[]{:S(2)}) copy-start(bf16[1152,1152]{1,0:T(8,128)(2,1)} %param.10) | copy-start | bytes 7962628
  7.2 100.6 %all-gather.2.cloned.1.call-start = ((), (), s32[]{:S(2)}) async-start(), calls=%async_computation.1 | async-start | bytes 11796480 | tf_op jit(solution)/shard_map/all_gather | solution.py:87
  13.1 290.5 %all-reduce.6.cloned.1.call-start = ((), (), s32[]{:S(2)}) async-start(), calls=%async_computation.4 | async-start | bytes 5308416
  22.5 2.1 copy-start.2
  34.0 4.6 %copy-start.8 = (f32[512,512]{0,1:T(8,128)}, f32[512,512]{0,1:T(8,128)S(1)}, u32[]{:S(2)}) copy-start(f32[512,512]{0,1:T(8,128)S(1)} %add_negate_fusion) | copy-start | bytes 3145732
  34.0 6.0 %copy-start.4 = (bf16[1024,1152]{1,0:T(8,128)(2,1)S(1)}, bf16[1024,1152]{1,0:T(8,128)(2,1)}, u32[]{:S(2)}) copy-start(bf16[1024,1152]{1,0:T(8,128)(2,1)} %fusion.4) | copy-start | bytes 7077892
  38.6 1.4 copy-start.7
  116.8 14.5 %copy-start.5 = (bf16[8,512,1152]{2,1,0:T(8,128)(2,1)S(1)}, bf16[8,512,1152]{2,1,0:T(8,128)(2,1)}, u32[]{:S(2)}) copy-start(bf16[8,512,1152]{2,1,0:T(8,128)(2,1)} %gather_fusion.1) | copy-start | bytes 28311556
  179.4 5.1 %copy-start.1 = (f32[2,512,1152]{2,1,0:T(8,128)S(1)}, f32[2,512,1152]{2,1,0:T(8,128)}, u32[]{:S(2)}) copy-start(f32[2,512,1152]{2,1,0:T(8,128)} %scatter_fusion) | copy-start | bytes 14155780
  184.5 5.3 %copy-start.9 = (bf16[1024,1152]{1,0:T(8,128)(2,1)S(1)}, bf16[1024,1152]{1,0:T(8,128)(2,1)}, u32[]{:S(2)}) copy-start(bf16[1024,1152]{1,0:T(8,128)(2,1)} %param.8) | copy-start | bytes 7077892
  188.3 1.4 copy-start.6
  189.7 4.9 %copy-start.10 = (u32[128]{0:T(128)S(1)}, u32[128]{0:T(128)}, u32[]{:S(2)}) copy-start(u32[128]{0:T(128)} %constant.54) | copy-start | bytes 1540
  194.6 172.3 %all-reduce.4.cloned.1.call-start = ((), (), s32[]{:S(2)}) async-start(), calls=%async_computation.3 | async-start | bytes 589824 | tf_op jit(solution)/shard_map/psum | solution.py:131
  305.6 134.6 %reduce-scatter.3.cloned.1.call-start = ((), (), s32[]{:S(2)}) async-start(), calls=%async_computation.2 | async-start | bytes 11796480 | tf_op jit(solution)/shard_map/reduce_scatter | solution.py:104
  440.2 5.2 %copy-start.3 = (bf16[1024,1152]{1,0:T(8,128)(2,1)S(1)}, bf16[1024,1152]{1,0:T(8,128)(2,1)}, u32[]{:S(2)}) copy-start(bf16[1024,1152]{1,0:T(8,128)(2,1)} %param.9) | copy-start | bytes 7077892
Sparse Core Ops, SparseCore 0:
  13.3 94.5 all-gather.1
  194.7 108.8 all-reduce.5
  306.1 42.0 all-reduce.3
  350.6 89.5 reduce-scatter.2
where the time goes:
time: 457 us; the launch traced here: 455 us
  waiting for transfers between devices  243 us (53%)
  other arithmetic  87.9 us (19%)
  matrix products  73.4 us (16%)
  local copies, waits for them, and re-layouts  34.4 us (8%)
  between operations  15.9 us (3%)
    unnamed x5, waiting for transfers between devices  108 us
    reduce_scatter x1, waiting for transfers between devices, per_device(): lax.psum_scatter(partial_value.reshape(groups * blocks * BLK, width), 'gr...  71.5 us
    all_gather x1, waiting for transfers between devices, per_device(): lax.all_gather(caption_segments, 'grp', axis=0, tiled=True)  64 us
    scatter-add x1, other arithmetic, per_device(): image_grads = image_grads.at[picture_position].add(hard_image)  32.7 us
    scatter-add x1, other arithmetic, per_device(): partial_value = jnp.zeros((groups * blocks, BLK, width), jnp.bfloat16).at...  24.3 us
    dot_general x2, matrix products, patch_contributions(): jnp.dot(derivative_patch, caption_segment, preferred_element_type=jnp.flo...  19.1 us
    dot_general x2, matrix products, patch_contributions(): jnp.dot(picture_segment, caption_segment.T, preferred_element_type=jnp.fl...  19.1 us
    dot_general x2, matrix products, patch_contributions(): jnp.dot(derivative_patch.T, picture_segment, preferred_element_type=jnp.f...  18.2 us
  transfers between devices with their start and end apart: 4, of which 3 were waited for; matrix products, arithmetic and copies ran while one was open for 20% of the time, Pallas kernels for 0%

commit v1 on v0

v1 whole, which is shorter than its diff:
```python
import functools

import jax
import jax.numpy as jnp
from jax import lax
from jax.experimental import pallas as pl
from jax.experimental.pallas import tpu as pltpu
from jax.sharding import PartitionSpec as P

MESH = pl.DeviceIdType.MESH
BLK = 512
D = 1152
ROWS = 1024
CH = 256
NCH = ROWS // CH
EPS = 1e-06
HR = 36
HP = 48
LO = 512
HI = D - LO
BF = jnp.bfloat16
F32 = jnp.float32

NN = (((1,), (0,)), ((), ()))
NT = (((1,), (1,)), ((), ()))
TN = (((0,), (0,)), ((), ()))


def mm(a, b, dims):
    return lax.dot_general(a, b, dims, preferred_element_type=F32)


def kernel(
    f_hbm, t_hbm, w_hbm, scale_ref, offset_ref, img_ref, cap_ref, cnt_ref,
    loss_out, pooled_out, text_out, head_out,
    fn, fp, tn, tun, tq, w, iun, iup, unit32, din, wide, si, st, ri, rt, gs, ep,
    hs, rc, rx, ry, ba, bb, r2a, r2b, zs, zr, inv_i, inv_t, loss_n, loss_p, ls, lr,
    f_send, f_recv, t_send, t_recv, di_send, di_recv, dt_send, dt_recv,
    l_sem, c_sem, x_send, x_recv, y_send, y_recv, x2_send, x2_recv, y2_send, y2_recv,
    z_send, z_recv, in_sem, out_sem,
):
    me = lax.axis_index("grp")
    inner = lax.axis_index("inner")
    odd = lax.rem(me, 2)
    gp = lax.rem(me + 3 + 2 * odd, 4)
    gq = lax.rem(me + 1 + 2 * odd, 4)
    core = lax.rem(inner, 2)
    x = lax.rem(inner // 2, 4)
    y = inner // 8

    def at(yy, xx, cc):
        return (yy * 4 + xx) * 2 + cc

    p_dev, q_dev = (gp, inner), (gq, inner)
    c_dev = (me, at(y, x, 1 - core))
    xs = [lax.rem(x + d, 4) for d in (1, 2, 3)]
    ys = [lax.rem(y + d, 4) for d in (1, 2, 3)]
    x_devs = [(me, at(y, v, core)) for v in xs]
    y_devs = [(me, at(v, x, core)) for v in ys]

    def remote(src, dst, send, recv, dev):
        return pltpu.make_async_remote_copy(
            src_ref=src, dst_ref=dst, send_sem=send, recv_sem=recv, device_id=dev, device_id_type=MESH
        )

    barrier = pltpu.get_barrier_semaphore()
    peers = [p_dev, q_dev, c_dev] + x_devs + y_devs
    for dev in peers:
        pl.semaphore_signal(barrier, inc=1, device_id=dev, device_id_type=MESH)
    pl.semaphore_wait(barrier, len(peers))

    def rows(c):
        return pl.ds(pl.multiple_of(c * CH, CH), CH)

    def half(c):
        return pl.ds(pl.multiple_of(lax.rem(c, 2) * CH, CH), CH)

    def f_copy(c):
        return remote(f_hbm.at[rows(c)], fp.at[rows(c)], f_send.at[c], f_recv.at[c], p_dev)

    def t_copy(c):
        return remote(t_hbm.at[rows(c)], tq.at[c // 2, half(c)], t_send.at[c], t_recv.at[c], q_dev)

    def di_copy(c):
        return remote(si.at[rows(c)], ri.at[rows(c)], di_send.at[c], di_recv.at[c], p_dev)

    def dt_copy(c):
        return remote(st.at[rows(c)], rt.at[rows(c)], dt_send.at[c], dt_recv.at[c], q_dev)

    for c in range(NCH):
        f_copy(c).start()
        t_copy(c).start()
    w_in = pltpu.make_async_copy(w_hbm, w, in_sem.at[0])
    f_in = pltpu.make_async_copy(f_hbm, fn, in_sem.at[1])
    t_in = pltpu.make_async_copy(t_hbm, tn, in_sem.at[2])
    w_in.start()
    f_in.start()
    t_in.start()

    scale = scale_ref[0]
    offset = offset_ref[0]

    def pair(g, h):
        first = cap_ref[g, 0, h, 0]
        a0, a1, live = img_ref[g, 0, h, 0], img_ref[g, 0, h, 1], cnt_ref[g, 0, h]
        out = []
        for k in range(2):
            slot = jnp.abs(first - k)
            out.append((a0 + (a1 - a0) * slot, jnp.clip(live - slot, 0, 1).astype(F32)))
        return out

    pair_a, pair_b, pair_c = pair(gp, me), pair(me, gq), pair(gp, gq)

    def hit(sel, b):
        return (1 - jnp.abs(sel - b)).astype(F32)

    def norm(v):
        return lax.rsqrt(jnp.sum(v * v, axis=-1, keepdims=True) + EPS)

    def project(g, u, inv):
        return (g - u * jnp.sum(g * u, axis=-1, keepdims=True)) * inv

    def loop(n, body, start=0):
        lax.fori_loop(start, n, lambda i, _: (body(i), 0)[1], 0)

    def embed(f_ref, c):
        e = mm(f_ref[rows(c), :], w[...], NN)
        inv = norm(e)
        return e * inv, inv

    w_in.wait()
    f_in.wait()

    def embed_own(c):
        unit, inv = embed(fn, c)
        unit32[rows(c), :] = unit
        inv_i[rows(c), :] = inv
        iun[c // 2, half(c), :] = unit.astype(BF)

    loop(NCH, embed_own)
    t_in.wait()

    def text_own(c):
        v = tn[rows(c), :].astype(F32)
        inv = norm(v)
        inv_t[rows(c), :] = inv
        tun[c // 2, half(c), :] = (v * inv).astype(BF)

    loop(NCH, text_own)

    def tile(images, sel, texts, k, slot, live, diagonal):
        def body(r):
            s = mm(images[sel, half(r), :], texts[k], NT) * scale + offset
            if diagonal:
                on = (lax.broadcasted_iota(jnp.int32, s.shape, 0) + r * CH) == lax.broadcasted_iota(jnp.int32, s.shape, 1)
                s = jnp.where(on, -s, s)
            e = jnp.exp(s)
            g = e / (1.0 + e)
            if diagonal:
                g = jnp.where(on, -g, g)
            else:
                g = g * live
            gs[slot, half(r), :] = g.astype(BF)
            total = jnp.sum(jnp.log1p(e), axis=1, keepdims=True)
            return total

        return body

    def tile_diag(k):
        body = tile(iun, k, tun, k, k, None, True)

        def step(r):
            loss_n[k, half(r), :] = body(r)

        loop(2, step)

    def tile_hard(images, texts, pr, k, slot, acc, first=False):
        sel, live = pr[k]
        body = tile(images, sel, texts, k, slot, live, False)

        def step(r):
            total = body(r) * live
            for b in range(2):
                v = total * hit(sel, b)
                if first:
                    acc[b, half(r), :] = v
                else:
                    acc[b, half(r), :] = acc[b, half(r), :] + v

        loop(2, step)

    loop(2, tile_diag)

    def arrive(c):
        f_copy(c).wait_recv()
        unit, _ = embed(fp, c)
        iup[c // 2, half(c), :] = unit.astype(BF)
        t_copy(c).wait_recv()
        v = tq[c // 2, half(c), :].astype(F32)
        tq[c // 2, half(c), :] = (v * norm(v)).astype(BF)

    loop(2, arrive)
    tile_hard(iun, tq, pair_b, 0, 4, loss_n)
    loop(4, arrive, 2)

    def back_text(c, parts):
        cols = half(c)
        out = None
        for slot, images, sel in parts:
            v = mm(gs[slot, :, cols], images[sel], TN)
            out = v if out is None else out + v
        return out * scale

    def back_image(c, parts):
        b = c // 2
        out = None
        for slot, texts, k, sel in parts:
            g = gs[slot, half(c), :]
            if sel is not None:
                g = (g.astype(F32) * hit(sel, b)).astype(BF)
            v = mm(g, texts[k], NN)
            out = v if out is None else out + v
        return out * scale

    def send_text(k):
        def step(c):
            st[rows(c), :] = back_text(c, ((4 + k, iun, pair_b[k][0]), (6 + k, iup, pair_c[k][0]))).astype(BF)
            dt_copy(c).start()

        loop(2 * k + 2, step, 2 * k)

    tile_hard(iup, tq, pair_c, 0, 6, loss_p, True)
    send_text(0)
    tile_hard(iup, tun, pair_a, 0, 2, loss_p)
    tile_hard(iup, tun, pair_a, 1, 3, loss_p)
    tile_hard(iup, tq, pair_c, 1, 7, loss_p)

    def send_image(c):
        g = back_image(
            c,
            ((2, tun, 0, pair_a[0][0]), (3, tun, 1, pair_a[1][0]), (6, tq, 0, pair_c[0][0]), (7, tq, 1, pair_c[1][0])),
        )
        si[rows(c), :] = g.astype(BF)
        di_copy(c).start()
        unit, inv = embed(fp, c)
        ep[rows(c), :] = project(g, unit, inv).astype(BF)

    loop(NCH, send_image)

    def row_form(ref, out):
        for i in range(8):
            v = ref[i // 4, pl.ds((i % 4) * 128, 128), :]
            out[pl.ds(i, 1), :] = jnp.transpose(jnp.broadcast_to(v, (128, 128)))[0:1, :]

    row_form(loss_p, ls)
    l_copy = remote(ls, lr, l_sem.at[0], l_sem.at[1], p_dev)
    l_copy.start()
    tile_hard(iun, tq, pair_b, 1, 5, loss_n)
    send_text(1)

    def own_image(c):
        b = c // 2
        g = mm(gs[b, half(c), :], tun[b], NN) * scale
        g = g + back_image(c, ((4, tq, 0, pair_b[0][0]), (5, tq, 1, pair_b[1][0])))
        din[rows(c), :] = g

    loop(NCH, own_image)

    def own_embed_grad(c):
        tq[c // 2, half(c), :] = project(din[rows(c), :], unit32[rows(c), :], inv_i[rows(c), :]).astype(BF)

    loop(NCH, own_embed_grad)

    def head(j):
        cols = pl.ds(pl.multiple_of(j * 384, 128), 384)
        h = mm(fp[:, cols], ep[...], TN)
        h = h + mm(fn[pl.ds(0, BLK), cols], tq[0], TN) + mm(fn[pl.ds(BLK, BLK), cols], tq[1], TN)
        wide[pl.ds(pl.multiple_of(j * 384, 128), 384), :] = h

    loop(3, head)

    zero = jnp.zeros((HP - HR, D), F32)

    def split(j):
        v = wide[pl.ds(pl.multiple_of(j * 2 * HR, 8), 2 * HR), :]
        for c in range(2):
            hs[j, c] = jnp.concatenate([v[c * HR : (c + 1) * HR, :], zero], axis=0).astype(BF)

    loop(16, split)
    c_copy = remote(hs.at[:, 1 - core], rc, c_sem.at[0], c_sem.at[1], c_dev)
    c_copy.start()

    def own_text(c):
        b = c // 2
        sel = jnp.where(b == 0, pair_a[0][0], pair_a[1][0])
        v = mm(gs[b, :, half(c)], iun[b], TN) + mm(gs[2 + b, :, half(c)], iup[sel], TN)
        wide[rows(c), :] = v * scale

    loop(NCH, own_text)

    c_copy.wait()

    def add_core(j):
        rc[j] = (rc[j].astype(F32) + hs[j, core].astype(F32)).astype(BF)

    loop(16, add_core)

    xc = []
    yc = []
    for d in range(3):
        xc += [
            remote(
                rc.at[pl.ds(yy * 4 + xs[d], 1), :, pl.ds(0, LO)], rx.at[d, pl.ds(yy, 1)],
                x_send.at[d, yy], x_recv.at[d, yy], x_devs[d],
            )
            for yy in range(4)
        ]
        yc.append(
            remote(
                rc.at[pl.ds(ys[d] * 4, 4), :, pl.ds(LO, HI)], ry.at[d],
                y_send.at[d], y_recv.at[d], y_devs[d],
            )
        )
    for copy in xc + yc:
        copy.start()

    def finish(c):
        di_copy(c).wait_recv()
        g = din[rows(c), :] + ri[rows(c), :].astype(F32)
        eg = project(g, unit32[rows(c), :], inv_i[rows(c), :]).astype(BF)
        iup[c // 2, half(c), :] = mm(eg, w[...], NT).astype(BF)
        pltpu.make_async_copy(iup.at[c // 2, half(c)], pooled_out.at[rows(c)], out_sem.at[0, c]).start()
        dt_copy(c).wait_recv()
        inv = inv_t[rows(c), :]
        u = tn[rows(c), :].astype(F32) * inv
        gt = wide[rows(c), :] + rt[rows(c), :].astype(F32)
        iun[c // 2, half(c), :] = project(gt, u, inv).astype(BF)
        pltpu.make_async_copy(iun.at[c // 2, half(c)], text_out.at[rows(c)], out_sem.at[1, c]).start()

    loop(2, finish)

    for copy in xc + yc:
        copy.wait()

    def add_x(yy):
        v = rc[yy * 4 + x, :, pl.ds(0, LO)].astype(F32)
        for d in range(3):
            v = v + rx[d, yy].astype(F32)
        ba[yy] = v.astype(BF)

    def add_y(xx):
        v = rc[y * 4 + xx, :, pl.ds(LO, HI)].astype(F32)
        for d in range(3):
            v = v + ry[d, xx].astype(F32)
        bb[xx] = v.astype(BF)

    loop(4, add_x)
    loop(4, add_y)
    second = []
    for d in range(3):
        second.append(remote(ba.at[ys[d]], r2a.at[d], y2_send.at[d], y2_recv.at[d], y_devs[d]))
        second.append(remote(bb.at[xs[d]], r2b.at[d], x2_send.at[d], x2_recv.at[d], x_devs[d]))
    for copy in second:
        copy.start()
    loop(3, finish, 2)
    for copy in second:
        copy.wait()
    lo = ba[y].astype(F32)
    hi = bb[x].astype(F32)
    for d in range(3):
        lo = lo + r2a[d].astype(F32)
        hi = hi + r2b[d].astype(F32)
    zs[0, :, pl.ds(0, LO)] = lo.astype(BF)
    zs[0, :, pl.ds(LO, HI)] = hi.astype(BF)
    z0 = remote(zs.at[0], zr.at[0], z_send.at[0], z_recv.at[0], p_dev)
    z0.start()
    z0.wait()
    zs[1] = (zs[0].astype(F32) + zr[0].astype(F32)).astype(BF)
    z1 = remote(zs.at[1], zr.at[1], z_send.at[1], z_recv.at[1], q_dev)
    z1.start()
    loop(4, finish, 3)
    l_copy.wait()
    row_form(loss_n, ls)
    loss_out[...] = (ls[...] + lr[...]) * (1.0 / BLK)
    z1.wait()
    head_out[...] = (zs[1].astype(F32) + zr[1].astype(F32))[0:HR, :]

    def drain(c):
        f_copy(c).wait_send()
        t_copy(c).wait_send()
        di_copy(c).wait_send()
        dt_copy(c).wait_send()
        pltpu.make_async_copy(iup.at[c // 2, half(c)], pooled_out.at[rows(c)], out_sem.at[0, c]).wait()
        pltpu.make_async_copy(iun.at[c // 2, half(c)], text_out.at[rows(c)], out_sem.at[1, c]).wait()

    loop(NCH, drain)


def per_device(features, captions, head, scaling, offset, img, cap, cnt):
    hbm = pl.BlockSpec(memory_space=pl.ANY)
    smem = pl.BlockSpec(memory_space=pltpu.SMEM)
    vmem = pl.BlockSpec(memory_space=pltpu.VMEM)
    big = pltpu.VMEM((ROWS, D), BF)
    blocks = pltpu.VMEM((2, BLK, D), BF)
    column = pltpu.VMEM((ROWS, 1), F32)
    dma = pltpu.SemaphoreType.DMA
    loss, pooled, text, grad = pl.pallas_call(
        kernel,
        out_shape=(
            jax.ShapeDtypeStruct((8, 128), F32),
            jax.ShapeDtypeStruct((ROWS, D), BF),
            jax.ShapeDtypeStruct((ROWS, D), BF),
            jax.ShapeDtypeStruct((HR, D), F32),
        ),
        in_specs=[hbm] * 3 + [smem] * 5,
        out_specs=(vmem, hbm, hbm, vmem),
        scratch_shapes=[
            big, big, big, blocks, blocks, pltpu.VMEM((D, D), BF), blocks, blocks,
            pltpu.VMEM((ROWS, D), F32), pltpu.VMEM((ROWS, D), F32), pltpu.VMEM((D, D), F32),
            big, big, big, big, pltpu.VMEM((8, BLK, BLK), BF), big,
            pltpu.VMEM((16, 2, HP, D), BF), pltpu.VMEM((16, HP, D), BF),
            pltpu.VMEM((3, 4, HP, LO), BF), pltpu.VMEM((3, 4, HP, HI), BF),
            pltpu.VMEM((4, HP, LO), BF), pltpu.VMEM((4, HP, HI), BF),
            pltpu.VMEM((3, HP, LO), BF), pltpu.VMEM((3, HP, HI), BF),
            pltpu.VMEM((2, HP, D), BF), pltpu.VMEM((2, HP, D), BF),
            column, column, pltpu.VMEM((2, BLK, 1), F32), pltpu.VMEM((2, BLK, 1), F32),
            pltpu.VMEM((8, 128), F32), pltpu.VMEM((8, 128), F32),
            dma((NCH,)), dma((NCH,)), dma((NCH,)), dma((NCH,)), dma((NCH,)), dma((NCH,)), dma((NCH,)), dma((NCH,)),
            dma((2,)), dma((2,)), dma((3, 4)), dma((3, 4)), dma((3,)), dma((3,)), dma((3,)), dma((3,)), dma((3,)), dma((3,)),
            dma((2,)), dma((2,)), dma((3,)), dma((2, NCH)),
        ],
        compiler_params=pltpu.CompilerParams(
            collective_id=0, has_side_effects=True, vmem_limit_bytes=63 << 20
        ),
        cost_estimate=pl.CostEstimate(flops=34_000_000_000, bytes_accessed=20_000_000, transcendentals=6_000_000),
    )(features, captions, head, scaling, offset, img, cap, cnt)
    return loss.reshape(ROWS), pooled, text, grad


def solution(mesh):
    return jax.shard_map(
        per_device,
        mesh=mesh,
        in_specs=(
            P(("grp", "inner"), None),
            P(("grp", "inner"), None),
            P(),
            P(),
            P(),
            P(None, "inner", None, None),
            P(None, "inner", None, None),
            P(None, "inner", None),
        ),
        out_specs=(
            P(("grp", "inner")),
            P(("grp", "inner"), None),
            P(("grp", "inner"), None),
            P("inner", None),
        ),
        check_vma=False,
    )
```

time: 457 us -> 142 us (0.31)
  waiting for transfers between devices: 243 us -> 0 us
  Pallas kernels: 0 us -> 130 us
  other arithmetic: 87.9 us -> 0 us
  matrix products: 73.4 us -> 0 us
  local copies, waits for them, and re-layouts: 34.4 us -> 9.52 us
  between operations: 15.9 us -> 1.94 us
    pallas_call x0 -> x1, Pallas kernels: none -> 130 us  [per_device(): pl.pallas_call(kernel, out_shape=(jax.ShapeDtypeStruct((8, 128), F32), ja...]
    unnamed x5 -> x0, waiting for transfers between devices: 108 us -> none
    dot_general x9 -> x0, matrix products: 73.4 us -> none  [the longest x2 19.1 us: patch_contributions(): jnp.dot(derivative_patch, caption_segment, preferred_element_type=jnp.flo...]
    reduce_scatter x1 -> x0, waiting for transfers between devices: 71.5 us -> none  [per_device(): lax.psum_scatter(partial_value.reshape(groups * blocks * BLK, width), 'gr...]
    all_gather x1 -> x0, waiting for transfers between devices: 64 us -> none  [per_device(): lax.all_gather(caption_segments, 'grp', axis=0, tiled=True)]
    scatter-add x3 -> x0, other arithmetic: 58 us -> none  [the longest x1 32.7 us: per_device(): image_grads = image_grads.at[picture_position].add(hard_image)]
    reduce_sum x5 -> x0, other arithmetic: 18.2 us -> none  [the longest x2 10.6 us: patch_contributions(): jnp.sum(jax.nn.softplus(-label_sign * similarity_scores_raw), axis=1)]
    gather x2 -> x0, local copies, waits for them, and re-layouts: 16.5 us -> none  [the longest x1 9 us: per_device(): collected_entries[caption_position]]
  transfers between devices with their start and end apart: 4 -> 0, of which waited for: 3 -> 0; matrix products, arithmetic and copies ran while one was open for 20% -> 0% of each run, Pallas kernels for 0% -> 0%
where the time goes in v1:
time: 142 us
  Pallas kernels  130 us (92%)
  local copies, waits for them, and re-layouts  9.52 us (7%)
  between operations  1.94 us (1%)
    pallas_call x1, Pallas kernels, per_device(): pl.pallas_call(kernel, out_shape=(jax.ShapeDtypeStruct((8, 128), F32), ja...  130 us
    unnamed x10, local copies, waits for them, and re-layouts  9.52 us

profile of v1, /device:TPU:0, one launch (start us, length us, event | category | flops | bytes accessed | tf_op | source)
XLA Modules:
  0.0 141.8 jit_solution(16135932926318351973)
XLA Ops:
  1.9 1.4 copy.12.img_ref
  3.3 1.4 copy.13.cap_ref
  4.7 130.3 %shard_map.111 = (f32[8,128]{1,0:T(8,128)}, bf16[1024,1152]{1,0:T(8,128)(2,1)}, bf16[1024,1152]{1,0:T(8,128)(2,1)}, f32[36,1152]{1,0:T(8,128)}) custom-call(bf16[1024,1152]{1,0:T(8,128)(2,1)} %f_hbm.1, bf16[1024,1152]{1,0:T(8,128)(2,1)} %t_hbm.1, bf16[1152,1152]{1,0:T(8,128)(2,1)} %w_hbm.1, f32[1]{0:T(128)S(6)} %copy.18.scale_ref, f32[1]{0:T(128)S(6)} %copy.19.offset_ref, ...), custom_call_target="tpu_custom_call" | custom-call | flops 33999998976 | bytes 20000000 | tf_op jit(solution)/shard_map/pallas_call | solution.py:407
  135.0 1.3 copy.20
  136.3 0.0 copy-start
  136.3 3.4 %copy.21 = bf16[1024,1152]{1,0:T(8,128)(2,1)} copy(bf16[1024,1152]{1,0:T(8,128)(2,1)} %get-tuple-element.17) | data formatting | bytes 4718592
  139.7 0.0 copy-done
  139.7 0.0 copy-start.1
  139.7 1.4 copy.22
  141.1 0.0 copy-done.1
  141.1 0.7 copy.23
Async XLA Ops:
  136.3 3.4 %copy-start = (bf16[1024,1152]{1,0:T(8,128)(2,1)S(1)}, bf16[1024,1152]{1,0:T(8,128)(2,1)}, u32[]{:S(2)}) copy-start(bf16[1024,1152]{1,0:T(8,128)(2,1)} %get-tuple-element.18) | copy-start | bytes 7077892
  139.7 1.4 copy-start.1

commit v2 on v1

v2 whole, which is shorter than its diff:
```python
import functools

import jax
import jax.numpy as jnp
from jax import lax
from jax.experimental import pallas as pl
from jax.experimental.pallas import tpu as pltpu
from jax.sharding import PartitionSpec as P

MESH = pl.DeviceIdType.MESH
BLK = 512
D = 1152
ROWS = 1024
CH = 256
NCH = ROWS // CH
SM = 128
NSM = ROWS // SM
EPS = 1e-06
HR = 36
HP = 48
LO = 512
HI = D - LO
BF = jnp.bfloat16
F32 = jnp.float32

NN = (((1,), (0,)), ((), ()))
NT = (((1,), (1,)), ((), ()))
TN = (((0,), (0,)), ((), ()))


def mm(a, b, dims):
    return lax.dot_general(a, b, dims, preferred_element_type=F32)


def kernel(
    f_hbm, t_hbm, w_hbm, scale_ref, offset_ref, img_ref, cap_ref, cnt_ref,
    loss_out, pooled_out, text_out, head_out,
    fn, fp, tn, tun, tq, w, iun, iup, unit32, din, wide, si, st, ri, rt, gs, ep,
    hs_lo, hs_hi, rc_lo, rc_hi, rx, ry, ba, bb, r2a, r2b, zs, zr, inv, loss_n, loss_p, ls, lr,
    f_send, f_recv, t_send, t_recv, di_send, di_recv, dt_send, dt_recv,
    l_sem, c_sem, x_send, x_recv, y_send, y_recv, x2_send, x2_recv, y2_send, y2_recv,
    z_send, z_recv, in_sem, out_sem,
):
    me = lax.axis_index("grp")
    inner = lax.axis_index("inner")
    odd = lax.rem(me, 2)
    gp = lax.rem(me + 3 + 2 * odd, 4)
    gq = lax.rem(me + 1 + 2 * odd, 4)
    core = lax.rem(inner, 2)
    x = lax.rem(inner // 2, 4)
    y = inner // 8

    def at(yy, xx, cc):
        return (yy * 4 + xx) * 2 + cc

    p_dev, q_dev = (gp, inner), (gq, inner)
    c_dev = (me, at(y, x, 1 - core))
    xs = [lax.rem(x + d, 4) for d in (1, 2, 3)]
    ys = [lax.rem(y + d, 4) for d in (1, 2, 3)]
    x_devs = [(me, at(y, v, core)) for v in xs]
    y_devs = [(me, at(v, x, core)) for v in ys]

    def remote(src, dst, send, recv, dev):
        return pltpu.make_async_remote_copy(
            src_ref=src, dst_ref=dst, send_sem=send, recv_sem=recv, device_id=dev, device_id_type=MESH
        )

    barrier = pltpu.get_barrier_semaphore()
    peers = [p_dev, q_dev, c_dev] + x_devs + y_devs
    for dev in peers:
        pl.semaphore_signal(barrier, inc=1, device_id=dev, device_id_type=MESH)
    pl.semaphore_wait(barrier, len(peers))

    def rows(c):
        return pl.ds(pl.multiple_of(c * CH, CH), CH)

    def half(c):
        return pl.ds(pl.multiple_of(lax.rem(c, 2) * CH, CH), CH)

    def small(c):
        return pl.ds(pl.multiple_of(c * SM, SM), SM)

    def part(c):
        return pl.ds(pl.multiple_of(lax.rem(c, 4) * SM, SM), SM)

    def f_copy(c):
        return remote(f_hbm.at[small(c)], fp.at[small(c)], f_send.at[c], f_recv.at[c], p_dev)

    def t_copy(c):
        return remote(t_hbm.at[small(c)], tq.at[c // 4, part(c)], t_send.at[c], t_recv.at[c], q_dev)

    def di_copy(c):
        return remote(si.at[rows(c)], ri.at[rows(c)], di_send.at[c], di_recv.at[c], p_dev)

    def dt_copy(c):
        return remote(st.at[rows(c)], rt.at[rows(c)], dt_send.at[c], dt_recv.at[c], q_dev)

    for c in range(NSM):
        f_copy(c).start()
        t_copy(c).start()
    w_in = pltpu.make_async_copy(w_hbm, w, in_sem.at[0])
    f_in = pltpu.make_async_copy(f_hbm, fn, in_sem.at[1])
    t_in = pltpu.make_async_copy(t_hbm, tn, in_sem.at[2])
    w_in.start()
    f_in.start()
    t_in.start()

    scale = scale_ref[0]
    offset = offset_ref[0]

    def pair(g, h):
        first = cap_ref[g, 0, 0, h]
        a0, a1, live = img_ref[g, 0, 0, h], img_ref[g, 0, 1, h], cnt_ref[g, 0, h]
        out = []
        for k in range(2):
            slot = jnp.abs(first - k)
            out.append((a0 + (a1 - a0) * slot, jnp.clip(live - slot, 0, 1).astype(F32)))
        return out

    pair_a, pair_b, pair_c = pair(gp, me), pair(me, gq), pair(gp, gq)

    def hit(sel, b):
        return (1 - jnp.abs(sel - b)).astype(F32)

    def norm(v):
        return lax.rsqrt(jnp.sum(v * v, axis=-1, keepdims=True) + EPS)

    def project(g, u, r):
        return (g - u * jnp.sum(g * u, axis=-1, keepdims=True)) * r

    def loop(n, body, start=0):
        lax.fori_loop(start, n, lambda i, _: (body(i), 0)[1], 0)

    def embed(f_ref, where):
        e = mm(f_ref[where, :], w[...], NN)
        r = norm(e)
        return e * r, r

    w_in.wait()
    f_in.wait()

    def embed_own(c):
        unit, r = embed(fn, rows(c))
        unit32[rows(c), :] = unit
        inv[rows(c), 0:1] = r
        iun[c // 2, half(c), :] = unit.astype(BF)

    loop(NCH, embed_own)
    t_in.wait()

    def text_own(c):
        v = tn[rows(c), :].astype(F32)
        r = norm(v)
        inv[rows(c), 2:3] = r
        tun[c // 2, half(c), :] = (v * r).astype(BF)

    loop(NCH, text_own)

    def tile(images, sel, texts, k, slot, live, diagonal):
        def body(r):
            s = mm(images[sel, half(r), :], texts[k], NT) * scale + offset
            if diagonal:
                on = (lax.broadcasted_iota(jnp.int32, s.shape, 0) + r * CH) == lax.broadcasted_iota(jnp.int32, s.shape, 1)
                s = jnp.where(on, -s, s)
            e = jnp.exp(s)
            g = e / (1.0 + e)
            if diagonal:
                g = jnp.where(on, -g, g)
            else:
                g = g * live
            gs[slot, half(r), :] = g.astype(BF)
            total = jnp.sum(jnp.log1p(e), axis=1, keepdims=True)
            return total

        return body

    def tile_diag(k):
        body = tile(iun, k, tun, k, k, None, True)

        def step(r):
            loss_n[k, half(r), :] = body(r)

        loop(2, step)

    def tile_hard(images, texts, pr, k, slot, acc, first=False):
        sel, live = pr[k]
        body = tile(images, sel, texts, k, slot, live, False)

        def step(r):
            total = body(r) * live
            for b in range(2):
                v = total * hit(sel, b)
                if first:
                    acc[b, half(r), :] = v
                else:
                    acc[b, half(r), :] = acc[b, half(r), :] + v

        loop(2, step)

    loop(2, tile_diag)

    def own_diag(c):
        b = c // 2
        din[rows(c), :] = mm(gs[b, half(c), :], tun[b], NN) * scale

    loop(NCH, own_diag)

    def arrive(c):
        b = c // 4
        f_copy(c).wait_recv()
        unit, r = embed(fp, small(c))
        wide[small(c), :] = unit
        inv[small(c), 1:2] = r
        u = unit.astype(BF)
        iup[b, part(c), :] = u
        total = None
        for k in range(2):
            sel, live = pair_a[k]
            keep = live * hit(sel, b)
            e = jnp.exp(mm(u, tun[k], NT) * scale + offset)
            gs[2 + 2 * k + b, part(c), :] = (e / (1.0 + e) * keep).astype(BF)
            v = jnp.sum(jnp.log1p(e), axis=1, keepdims=True) * keep
            total = v if total is None else total + v
        loss_p[b, part(c), :] = total
        t_copy(c).wait_recv()
        v = tq[b, part(c), :].astype(F32)
        tq[b, part(c), :] = (v * norm(v)).astype(BF)

    loop(4, arrive)
    tile_hard(iun, tq, pair_b, 0, 6, loss_n)

    def back_text(c, parts):
        cols = half(c)
        out = None
        for slot, images, sel in parts:
            v = mm(gs[slot, :, cols], images[sel], TN)
            out = v if out is None else out + v
        return out * scale

    def back_image(c, parts):
        b = c // 2
        out = None
        for slot, texts, k, sel in parts:
            g = gs[slot, half(c), :]
            if sel is not None:
                g = (g.astype(F32) * hit(sel, b)).astype(BF)
            v = mm(g, texts[k], NN)
            out = v if out is None else out + v
        return out * scale

    def own_first(c):
        din[rows(c), :] = din[rows(c), :] + back_image(c, ((6, tq, 0, pair_b[0][0]),))

    loop(NCH, own_first)
    loop(NSM, arrive, 4)

    def send_text(c):
        k = c // 2
        sel_b = jnp.where(k == 0, pair_b[0][0], pair_b[1][0])
        sel_c = jnp.where(k == 0, pair_c[0][0], pair_c[1][0])
        st[rows(c), :] = back_text(c, ((6 + k, iun, sel_b), (8 + k, iup, sel_c))).astype(BF)
        dt_copy(c).start()

    def send_image(c):
        b = c // 2
        g = back_image(
            c,
            ((2 + b, tun, 0, None), (4 + b, tun, 1, None), (8, tq, 0, pair_c[0][0]), (9, tq, 1, pair_c[1][0])),
        )
        si[rows(c), :] = g.astype(BF)
        di_copy(c).start()
        ep[rows(c), :] = project(g, wide[rows(c), :], inv[rows(c), 1:2]).astype(BF)

    tile_hard(iup, tq, pair_c, 0, 8, loss_p)
    loop(1, send_text)
    tile_hard(iup, tq, pair_c, 1, 9, loss_p)
    loop(1, send_image)
    loop(2, send_text, 1)
    loop(NCH, send_image, 1)

    def row_form(ref, out):
        for i in range(8):
            v = ref[i // 4, pl.ds((i % 4) * 128, 128), :]
            out[pl.ds(i, 1), :] = jnp.transpose(jnp.broadcast_to(v, (128, 128)))[0:1, :]

    row_form(loss_p, ls)
    l_copy = remote(ls, lr, l_sem.at[0], l_sem.at[1], p_dev)
    l_copy.start()
    tile_hard(iun, tq, pair_b, 1, 7, loss_n)

    def own_image(c):
        g = din[rows(c), :] + back_image(c, ((7, tq, 1, pair_b[1][0]),))
        din[rows(c), :] = g
        tun[c // 2, half(c), :] = project(g, unit32[rows(c), :], inv[rows(c), 0:1]).astype(BF)

    loop(NCH, own_image)

    def head(cols, hs):
        width = cols.size

        def step(j):
            own = pl.ds(pl.multiple_of(j * 384, 128), 384)
            h = mm(fp[:, own], ep[:, cols], TN)
            h = h + mm(fn[pl.ds(0, BLK), own], tun[0, :, cols], TN) + mm(fn[pl.ds(BLK, BLK), own], tun[1, :, cols], TN)
            wide[own, cols] = h

        loop(3, step)
        zero = jnp.zeros((HP - HR, width), F32)

        def split(j):
            v = wide[pl.ds(pl.multiple_of(j * 2 * HR, 8), 2 * HR), cols]
            for c in range(2):
                hs[j, c] = jnp.concatenate([v[c * HR : (c + 1) * HR, :], zero], axis=0).astype(BF)

        loop(16, split)

    lo_cols, hi_cols = pl.ds(0, LO), pl.ds(LO, HI)
    head(lo_cols, hs_lo)
    c_lo = remote(hs_lo.at[:, 1 - core], rc_lo, c_sem.at[0], c_sem.at[1], c_dev)
    c_lo.start()
    head(hi_cols, hs_hi)
    c_hi = remote(hs_hi.at[:, 1 - core], rc_hi, c_sem.at[2], c_sem.at[3], c_dev)
    c_hi.start()
    loop(NCH, send_text, 2)

    def add_core(rc, hs):
        def step(j):
            rc[j] = (rc[j].astype(F32) + hs[j, core].astype(F32)).astype(BF)

        loop(16, step)

    c_lo.wait()
    add_core(rc_lo, hs_lo)
    xc = []
    for d in range(3):
        xc += [
            remote(
                rc_lo.at[yy * 4 + xs[d]], rx.at[d, yy], x_send.at[d, yy], x_recv.at[d, yy], x_devs[d]
            )
            for yy in range(4)
        ]
    for copy in xc:
        copy.start()
    c_hi.wait()
    add_core(rc_hi, hs_hi)
    yc = [
        remote(rc_hi.at[pl.ds(ys[d] * 4, 4)], ry.at[d], y_send.at[d], y_recv.at[d], y_devs[d]) for d in range(3)
    ]
    for copy in yc:
        copy.start()

    def own_text(c):
        b = c // 2
        sel = jnp.where(b == 0, pair_a[0][0], pair_a[1][0])
        v = mm(gs[b, :, half(c)], iun[b], TN) + mm(gs[2 + 2 * b + sel, :, half(c)], iup[sel], TN)
        wide[rows(c), :] = v * scale

    loop(NCH, own_text)

    def finish(c):
        di_copy(c).wait_recv()
        g = din[rows(c), :] + ri[rows(c), :].astype(F32)
        eg = project(g, unit32[rows(c), :], inv[rows(c), 0:1]).astype(BF)
        iup[c // 2, half(c), :] = mm(eg, w[...], NT).astype(BF)
        pltpu.make_async_copy(iup.at[c // 2, half(c)], pooled_out.at[rows(c)], out_sem.at[0, c]).start()
        dt_copy(c).wait_recv()
        r = inv[rows(c), 2:3]
        u = tn[rows(c), :].astype(F32) * r
        gt = wide[rows(c), :] + rt[rows(c), :].astype(F32)
        iun[c // 2, half(c), :] = project(gt, u, r).astype(BF)
        pltpu.make_async_copy(iun.at[c // 2, half(c)], text_out.at[rows(c)], out_sem.at[1, c]).start()

    loop(2, finish)

    def add_x(yy):
        v = rc_lo[yy * 4 + x].astype(F32)
        for d in range(3):
            v = v + rx[d, yy].astype(F32)
        ba[yy] = v.astype(BF)

    def add_y(xx):
        v = rc_hi[y * 4 + xx].astype(F32)
        for d in range(3):
            v = v + ry[d, xx].astype(F32)
        bb[xx] = v.astype(BF)

    for copy in xc:
        copy.wait()
    loop(4, add_x)
    second = [remote(ba.at[ys[d]], r2a.at[d], y2_send.at[d], y2_recv.at[d], y_devs[d]) for d in range(3)]
    for copy in second:
        copy.start()
    for copy in yc:
        copy.wait()
    loop(4, add_y)
    third = [remote(bb.at[xs[d]], r2b.at[d], x2_send.at[d], x2_recv.at[d], x_devs[d]) for d in range(3)]
    for copy in third:
        copy.start()
    loop(3, finish, 2)
    for copy in second + third:
        copy.wait()
    lo = ba[y].astype(F32)
    hi = bb[x].astype(F32)
    for d in range(3):
        lo = lo + r2a[d].astype(F32)
        hi = hi + r2b[d].astype(F32)
    zs[0, :, pl.ds(0, LO)] = lo.astype(BF)
    zs[0, :, pl.ds(LO, HI)] = hi.astype(BF)
    z0 = remote(zs.at[0], zr.at[0], z_send.at[0], z_recv.at[0], p_dev)
    z0.start()
    z0.wait()
    zs[1] = (zs[0].astype(F32) + zr[0].astype(F32)).astype(BF)
    z1 = remote(zs.at[1], zr.at[1], z_send.at[1], z_recv.at[1], q_dev)
    z1.start()
    loop(4, finish, 3)
    l_copy.wait()
    row_form(loss_n, ls)
    loss_out[...] = (ls[...] + lr[...]) * (1.0 / BLK)
    z1.wait()
    head_out[...] = (zs[1].astype(F32) + zr[1].astype(F32))[0:HR, :]

    def sent(c):
        f_copy(c).wait_send()
        t_copy(c).wait_send()

    loop(NSM, sent)

    def drain(c):
        di_copy(c).wait_send()
        dt_copy(c).wait_send()
        pltpu.make_async_copy(iup.at[c // 2, half(c)], pooled_out.at[rows(c)], out_sem.at[0, c]).wait()
        pltpu.make_async_copy(iun.at[c // 2, half(c)], text_out.at[rows(c)], out_sem.at[1, c]).wait()

    loop(NCH, drain)


def emit(loss, pooled, text, grad, loss_out, pooled_out, text_out, grad_out, stage, small, sem_in, sem_out):
    reads, writes = [], []
    for c in range(NCH):
        for i, (src, dst) in enumerate(((pooled, pooled_out), (text, text_out))):
            where = pl.ds(c * CH, CH)
            reads.append(pltpu.make_async_copy(src.at[where], stage.at[i, where], sem_in.at[i, c]))
            writes.append(pltpu.make_async_copy(stage.at[i, where], dst.at[where], sem_out.at[i, c]))
    reads.append(pltpu.make_async_copy(grad, small, sem_in.at[2, 0]))
    writes.append(pltpu.make_async_copy(small, grad_out, sem_out.at[2, 0]))
    for copy in reads:
        copy.start()
    for i in range(8):
        loss_out[pl.ds(i * 128, 128)] = loss[i, :]
    for read, write in zip(reads, writes):
        read.wait()
        write.start()
    for copy in writes:
        copy.wait()


def per_device(features, captions, head, scaling, offset, img, cap, cnt):
    hbm = pl.BlockSpec(memory_space=pl.ANY)
    smem = pl.BlockSpec(memory_space=pltpu.SMEM)
    vmem = pl.BlockSpec(memory_space=pltpu.VMEM)
    big = pltpu.VMEM((ROWS, D), BF)
    blocks = pltpu.VMEM((2, BLK, D), BF)
    dma = pltpu.SemaphoreType.DMA
    loss, pooled, text, grad = pl.pallas_call(
        kernel,
        out_shape=(
            jax.ShapeDtypeStruct((8, 128), F32),
            jax.ShapeDtypeStruct((ROWS, D), BF),
            jax.ShapeDtypeStruct((ROWS, D), BF),
            jax.ShapeDtypeStruct((HR, D), F32),
        ),
        in_specs=[hbm] * 3 + [smem] * 5,
        out_specs=(vmem, hbm, hbm, vmem),
        scratch_shapes=[
            big, big, big, blocks, blocks, pltpu.VMEM((D, D), BF), blocks, blocks,
            pltpu.VMEM((ROWS, D), F32), pltpu.VMEM((ROWS, D), F32), pltpu.VMEM((D, D), F32),
            big, big, big, big, pltpu.VMEM((10, BLK, BLK), BF), big,
            pltpu.VMEM((16, 2, HP, LO), BF), pltpu.VMEM((16, 2, HP, HI), BF),
            pltpu.VMEM((16, HP, LO), BF), pltpu.VMEM((16, HP, HI), BF),
            pltpu.VMEM((3, 4, HP, LO), BF), pltpu.VMEM((3, 4, HP, HI), BF),
            pltpu.VMEM((4, HP, LO), BF), pltpu.VMEM((4, HP, HI), BF),
            pltpu.VMEM((3, HP, LO), BF), pltpu.VMEM((3, HP, HI), BF),
            pltpu.VMEM((2, HP, D), BF), pltpu.VMEM((2, HP, D), BF),
            pltpu.VMEM((ROWS, 3), F32), pltpu.VMEM((2, BLK, 1), F32), pltpu.VMEM((2, BLK, 1), F32),
            pltpu.VMEM((8, 128), F32), pltpu.VMEM((8, 128), F32),
            dma((NSM,)), dma((NSM,)), dma((NSM,)), dma((NSM,)), dma((NCH,)), dma((NCH,)), dma((NCH,)), dma((NCH,)),
            dma((2,)), dma((4,)), dma((3, 4)), dma((3, 4)), dma((3,)), dma((3,)), dma((3,)), dma((3,)), dma((3,)), dma((3,)),
            dma((2,)), dma((2,)), dma((3,)), dma((2, NCH)),
        ],
        compiler_params=pltpu.CompilerParams(
            collective_id=0, has_side_effects=True, vmem_limit_bytes=63 << 20
        ),
        cost_estimate=pl.CostEstimate(flops=34_000_000_000, bytes_accessed=20_000_000, transcendentals=6_000_000),
    )(features, captions, head, scaling, offset, jnp.swapaxes(img, 2, 3), jnp.swapaxes(cap, 2, 3), cnt)
    return pl.pallas_call(
        emit,
        out_shape=(
            jax.ShapeDtypeStruct((ROWS,), F32),
            jax.ShapeDtypeStruct((ROWS, D), BF),
            jax.ShapeDtypeStruct((ROWS, D), BF),
            jax.ShapeDtypeStruct((HR, D), F32),
        ),
        in_specs=[vmem, hbm, hbm, hbm],
        out_specs=(vmem, hbm, hbm, hbm),
        scratch_shapes=[pltpu.VMEM((2, ROWS, D), BF), pltpu.VMEM((HR, D), F32), dma((3, NCH)), dma((3, NCH))],
        compiler_params=pltpu.CompilerParams(vmem_limit_bytes=63 << 20),
    )(loss, pooled, text, grad)


def solution(mesh):
    return jax.shard_map(
        per_device,
        mesh=mesh,
        in_specs=(
            P(("grp", "inner"), None),
            P(("grp", "inner"), None),
            P(),
            P(),
            P(),
            P(None, "inner", None, None),
            P(None, "inner", None, None),
            P(None, "inner", None),
        ),
        out_specs=(
            P(("grp", "inner")),
            P(("grp", "inner"), None),
            P(("grp", "inner"), None),
            P("inner", None),
        ),
        check_vma=False,
    )
```

time: 142 us -> 133 us (0.937)
  local copies, waits for them, and re-layouts: 9.52 us -> 0 us
    unnamed x10 -> x0, local copies, waits for them, and re-layouts: 9.52 us -> none
    pallas_call x1, Pallas kernels: 130 us -> 124 us  [per_device(): pl.pallas_call(kernel, out_shape=(jax.ShapeDtypeStruct((8, 128), F32), ja...]
    pallas_call x0 -> x1, Pallas kernels: none -> 5.51 us  [per_device(): pl.pallas_call(emit, out_shape=(jax.ShapeDtypeStruct((ROWS,), F32), jax.S...]
where the time goes in v2:
time: 133 us; the launch traced here: 132 us
  Pallas kernels  130 us (98%)
  between operations  2.09 us (2%)
    pallas_call x1, Pallas kernels, per_device(): pl.pallas_call(kernel, out_shape=(jax.ShapeDtypeStruct((8, 128), F32), ja...  124 us
    pallas_call x1, Pallas kernels, per_device(): pl.pallas_call(emit, out_shape=(jax.ShapeDtypeStruct((ROWS,), F32), jax.S...  5.51 us

profile of v2, /device:TPU:0, one launch (start us, length us, event | category | flops | bytes accessed | tf_op | source)
XLA Modules:
  0.0 131.9 jit_solution(3119478774674390011)
XLA Ops:
  1.9 124.3 %shard_map.111 = (f32[8,128]{1,0:T(8,128)}, bf16[1024,1152]{1,0:T(8,128)(2,1)}, bf16[1024,1152]{1,0:T(8,128)(2,1)}, f32[36,1152]{1,0:T(8,128)}) custom-call(bf16[1024,1152]{1,0:T(8,128)(2,1)} %f_hbm.1, bf16[1024,1152]{1,0:T(8,128)(2,1)} %t_hbm.1, bf16[1152,1152]{1,0:T(8,128)(2,1)} %w_hbm.1, f32[1]{0:T(128)S(6)} %copy.12.scale_ref, f32[1]{0:T(128)S(6)} %copy.13.offset_ref, ...), custom_call_target="tpu_custom_call" | custom-call | flops 33999998976 | bytes 20000000 | tf_op jit(solution)/shard_map/pallas_call | solution.py:464
  126.2 5.5 %shard_map.112 = (f32[1024]{0:T(1024)}, bf16[1024,1152]{1,0:T(8,128)(2,1)}, bf16[1024,1152]{1,0:T(8,128)(2,1)}, f32[36,1152]{1,0:T(8,128)}) custom-call(f32[8,128]{1,0:T(8,128)} %get-tuple-element.8.loss, bf16[1024,1152]{1,0:T(8,128)(2,1)} %get-tuple-element.9.pooled, bf16[1024,1152]{1,0:T(8,128)(2,1)} %get-tuple-element.10.text, ...), custom_call_target="tpu_custom_call" | custom-call | tf_op jit(solution)/shard_map/pallas_call | solution.py:495

commit v3 on v2

--- a/solution.py
+++ b/solution.py
@@ -34,12 +34,12 @@
 
 def kernel(
     f_hbm, t_hbm, w_hbm, scale_ref, offset_ref, img_ref, cap_ref, cnt_ref,
-    loss_out, pooled_out, text_out, head_out,
-    fn, fp, tn, tun, tq, w, iun, iup, unit32, din, wide, si, st, ri, rt, gs, ep,
-    hs_lo, hs_hi, rc_lo, rc_hi, rx, ry, ba, bb, r2a, r2b, zs, zr, inv, loss_n, loss_p, ls, lr,
+    loss_out, iup, iun, head_out,
+    fn, fp, tn, tun, tq, w, unit32, din, wide, si, st, ri, rt, gs, ep,
+    hs_lo, hs_hi, rc_lo, rc_hi, rx, ry, ba, bb, r2a, r2b, zs, zr, inv, ls, lr,
     f_send, f_recv, t_send, t_recv, di_send, di_recv, dt_send, dt_recv,
     l_sem, c_sem, x_send, x_recv, y_send, y_recv, x2_send, x2_recv, y2_send, y2_recv,
-    z_send, z_recv, in_sem, out_sem,
+    z_send, z_recv, in_sem,
 ):
     me = lax.axis_index("grp")
     inner = lax.axis_index("inner")
@@ -90,10 +90,10 @@
         return remote(t_hbm.at[small(c)], tq.at[c // 4, part(c)], t_send.at[c], t_recv.at[c], q_dev)
 
     def di_copy(c):
-        return remote(si.at[rows(c)], ri.at[rows(c)], di_send.at[c], di_recv.at[c], p_dev)
+        return remote(si.at[small(c)], ri.at[small(c)], di_send.at[c], di_recv.at[c], p_dev)
 
     def dt_copy(c):
-        return remote(st.at[rows(c)], rt.at[rows(c)], dt_send.at[c], dt_recv.at[c], q_dev)
+        return remote(st.at[small(c)], rt.at[small(c)], dt_send.at[c], dt_recv.at[c], q_dev)
 
     for c in range(NSM):
         f_copy(c).start()
@@ -155,6 +155,9 @@
         tun[c // 2, half(c), :] = (v * r).astype(BF)
 
     loop(NCH, text_own)
+
+    def line(b, start, n):
+        return pl.ds(pl.multiple_of(b * BLK + start, SM), n)
 
     def tile(images, sel, texts, k, slot, live, diagonal):
         def body(r):
@@ -178,24 +181,29 @@
         body = tile(iun, k, tun, k, k, None, True)
 
         def step(r):
-            loss_n[k, half(r), :] = body(r)
+            inv[line(k, r * CH, CH), 3:4] = body(r)
 
         loop(2, step)
 
-    def tile_hard(images, texts, pr, k, slot, acc, first=False):
-        sel, live = pr[k]
-        body = tile(images, sel, texts, k, slot, live, False)
+    def tile_own(k, slot):
+        sel, live = pair_b[k]
+        body = tile(iun, sel, tq, k, slot, live, False)
 
         def step(r):
             total = body(r) * live
             for b in range(2):
-                v = total * hit(sel, b)
-                if first:
-                    acc[b, half(r), :] = v
-                else:
-                    acc[b, half(r), :] = acc[b, half(r), :] + v
+                where = line(b, r * CH, CH)
+                inv[where, 3:4] = inv[where, 3:4] + total * hit(sel, b)
 
         loop(2, step)
+
+    def piece(b, r0, nr, k, c0, nc):
+        sel, live = pair_c[k]
+        keep = live * hit(sel, b)
+        e = jnp.exp(mm(iup[b, r0 : r0 + nr, :], tq[k, c0 : c0 + nc, :], NT) * scale + offset)
+        gs[8 + 2 * k + b, r0 : r0 + nr, c0 : c0 + nc] = (e / (1.0 + e) * keep).astype(BF)
+        where = pl.ds(b * BLK + r0, nr)
+        inv[where, 4:5] = inv[where, 4:5] + jnp.sum(jnp.log1p(e), axis=1, keepdims=True) * keep
 
     loop(2, tile_diag)
 
@@ -221,13 +229,13 @@
             gs[2 + 2 * k + b, part(c), :] = (e / (1.0 + e) * keep).astype(BF)
             v = jnp.sum(jnp.log1p(e), axis=1, keepdims=True) * keep
             total = v if total is None else total + v
-        loss_p[b, part(c), :] = total
+        inv[small(c), 4:5] = total
         t_copy(c).wait_recv()
         v = tq[b, part(c), :].astype(F32)
         tq[b, part(c), :] = (v * norm(v)).astype(BF)
 
     loop(4, arrive)
-    tile_hard(iun, tq, pair_b, 0, 6, loss_n)
+    tile_own(0, 6)
 
     def back_text(c, parts):
         cols = half(c)
@@ -252,41 +260,59 @@
         din[rows(c), :] = din[rows(c), :] + back_image(c, ((6, tq, 0, pair_b[0][0]),))
 
     loop(NCH, own_first)
-    loop(NSM, arrive, 4)
-
-    def send_text(c):
+    piece(0, 0, 256, 0, 0, 512)
+    piece(0, 256, 256, 0, 0, 512)
+    loop(6, arrive, 4)
+    piece(1, 0, 256, 0, 0, 512)
+    piece(1, 0, 256, 1, 0, 256)
+    piece(0, 0, 512, 1, 0, 256)
+    loop(7, arrive, 6)
+    piece(1, 256, 128, 0, 0, 512)
+    piece(1, 256, 128, 1, 0, 384)
+    piece(0, 0, 512, 1, 256, 128)
+    piece(1, 0, 256, 1, 256, 128)
+    loop(NSM, arrive, 7)
+    piece(1, 384, 128, 0, 0, 512)
+    piece(1, 384, 128, 1, 0, 512)
+    piece(0, 0, 512, 1, 384, 128)
+    piece(1, 0, 384, 1, 384, 128)
+
+    def send_text(c, last=False):
         k = c // 2
         sel_b = jnp.where(k == 0, pair_b[0][0], pair_b[1][0])
         sel_c = jnp.where(k == 0, pair_c[0][0], pair_c[1][0])
-        st[rows(c), :] = back_text(c, ((6 + k, iun, sel_b), (8 + k, iup, sel_c))).astype(BF)
-        dt_copy(c).start()
-
-    def send_image(c):
+        st[rows(c), :] = back_text(c, ((6 + k, iun, sel_b), (8 + 2 * k + sel_c, iup, sel_c))).astype(BF)
+        dt_copy(2 * c).start()
+        if not last:
+            dt_copy(2 * c + 1).start()
+
+    def send_image(c, last=False):
         b = c // 2
         g = back_image(
             c,
-            ((2 + b, tun, 0, None), (4 + b, tun, 1, None), (8, tq, 0, pair_c[0][0]), (9, tq, 1, pair_c[1][0])),
+            ((2 + b, tun, 0, None), (4 + b, tun, 1, None), (8 + b, tq, 0, None), (10 + b, tq, 1, None)),
         )
         si[rows(c), :] = g.astype(BF)
-        di_copy(c).start()
+        di_copy(2 * c).start()
+        if not last:
+            di_copy(2 * c + 1).start()
         ep[rows(c), :] = project(g, wide[rows(c), :], inv[rows(c), 1:2]).astype(BF)
 
-    tile_hard(iup, tq, pair_c, 0, 8, loss_p)
+    loop(1, send_image)
     loop(1, send_text)
-    tile_hard(iup, tq, pair_c, 1, 9, loss_p)
-    loop(1, send_image)
+    loop(NCH - 1, send_image, 1)
+    loop(NCH, lambda c: send_image(c, True), NCH - 1)
     loop(2, send_text, 1)
-    loop(NCH, send_image, 1)
-
-    def row_form(ref, out):
+
+    def row_form(at_col, out):
         for i in range(8):
-            v = ref[i // 4, pl.ds((i % 4) * 128, 128), :]
+            v = inv[pl.ds(i * 128, 128), at_col : at_col + 1]
             out[pl.ds(i, 1), :] = jnp.transpose(jnp.broadcast_to(v, (128, 128)))[0:1, :]
 
-    row_form(loss_p, ls)
+    row_form(4, ls)
     l_copy = remote(ls, lr, l_sem.at[0], l_sem.at[1], p_dev)
     l_copy.start()
-    tile_hard(iun, tq, pair_b, 1, 7, loss_n)
+    tile_own(1, 7)
 
     def own_image(c):
         g = din[rows(c), :] + back_image(c, ((7, tq, 1, pair_b[1][0]),))
@@ -295,9 +321,7 @@
 
     loop(NCH, own_image)
 
-    def head(cols, hs):
-        width = cols.size
-
+    def head(cols, hs, by_y):
         def step(j):
             own = pl.ds(pl.multiple_of(j * 384, 128), 384)
             h = mm(fp[:, own], ep[:, cols], TN)
@@ -305,46 +329,42 @@
             wide[own, cols] = h
 
         loop(3, step)
-        zero = jnp.zeros((HP - HR, width), F32)
 
         def split(j):
-            v = wide[pl.ds(pl.multiple_of(j * 2 * HR, 8), 2 * HR), cols]
+            v = []
+            for i in range(4):
+                at_row = (j * 4 + i if by_y else i * 4 + j) * 2 * HR
+                v.append(wide[pl.ds(pl.multiple_of(at_row, 8), 2 * HR), cols])
             for c in range(2):
-                hs[j, c] = jnp.concatenate([v[c * HR : (c + 1) * HR, :], zero], axis=0).astype(BF)
-
-        loop(16, split)
+                hs[c, j] = jnp.concatenate([u[c * HR : (c + 1) * HR, :] for u in v], axis=0).astype(BF)
+
+        loop(4, split)
 
     lo_cols, hi_cols = pl.ds(0, LO), pl.ds(LO, HI)
-    head(lo_cols, hs_lo)
-    c_lo = remote(hs_lo.at[:, 1 - core], rc_lo, c_sem.at[0], c_sem.at[1], c_dev)
+    head(lo_cols, hs_lo, False)
+    c_lo = remote(hs_lo.at[1 - core], rc_lo, c_sem.at[0], c_sem.at[1], c_dev)
     c_lo.start()
-    head(hi_cols, hs_hi)
-    c_hi = remote(hs_hi.at[:, 1 - core], rc_hi, c_sem.at[2], c_sem.at[3], c_dev)
+    head(hi_cols, hs_hi, True)
+    c_hi = remote(hs_hi.at[1 - core], rc_hi, c_sem.at[2], c_sem.at[3], c_dev)
     c_hi.start()
-    loop(NCH, send_text, 2)
+    loop(NCH - 1, send_text, 2)
+    loop(NCH, lambda c: send_text(c, True), NCH - 1)
 
     def add_core(rc, hs):
         def step(j):
-            rc[j] = (rc[j].astype(F32) + hs[j, core].astype(F32)).astype(BF)
-
-        loop(16, step)
+            rc[j] = (rc[j].astype(F32) + hs[core, j].astype(F32)).astype(BF)
+
+        loop(4, step)
 
     c_lo.wait()
     add_core(rc_lo, hs_lo)
-    xc = []
-    for d in range(3):
-        xc += [
-            remote(
-                rc_lo.at[yy * 4 + xs[d]], rx.at[d, yy], x_send.at[d, yy], x_recv.at[d, yy], x_devs[d]
-            )
-            for yy in range(4)
-        ]
+    xc = [remote(rc_lo.at[xs[d]], rx.at[d], x_send.at[d], x_recv.at[d], x_devs[d]) for d in range(3)]
     for copy in xc:
         copy.start()
     c_hi.wait()
     add_core(rc_hi, hs_hi)
     yc = [
-        remote(rc_hi.at[pl.ds(ys[d] * 4, 4)], ry.at[d], y_send.at[d], y_recv.at[d], y_devs[d]) for d in range(3)
+        remote(rc_hi.at[ys[d]], ry.at[d], y_send.at[d], y_recv.at[d], y_devs[d]) for d in range(3)
     ]
     for copy in yc:
         copy.start()
@@ -357,42 +377,40 @@
 
     loop(NCH, own_text)
 
-    def finish(c):
-        di_copy(c).wait_recv()
-        g = din[rows(c), :] + ri[rows(c), :].astype(F32)
-        eg = project(g, unit32[rows(c), :], inv[rows(c), 0:1]).astype(BF)
-        iup[c // 2, half(c), :] = mm(eg, w[...], NT).astype(BF)
-        pltpu.make_async_copy(iup.at[c // 2, half(c)], pooled_out.at[rows(c)], out_sem.at[0, c]).start()
-        dt_copy(c).wait_recv()
-        r = inv[rows(c), 2:3]
-        u = tn[rows(c), :].astype(F32) * r
-        gt = wide[rows(c), :] + rt[rows(c), :].astype(F32)
-        iun[c // 2, half(c), :] = project(gt, u, r).astype(BF)
-        pltpu.make_async_copy(iun.at[c // 2, half(c)], text_out.at[rows(c)], out_sem.at[1, c]).start()
+    def finish(c, n=CH):
+        where = pl.ds(pl.multiple_of(c * n, SM), n)
+        inside = pl.ds(pl.multiple_of(lax.rem(c, BLK // n) * n, SM), n)
+        b = c // (BLK // n)
+        for i in range(n // SM):
+            di_copy(c * (n // SM) + i).wait_recv()
+        g = din[where, :] + ri[where, :].astype(F32)
+        eg = project(g, unit32[where, :], inv[where, 0:1]).astype(BF)
+        iup[b, inside, :] = mm(eg, w[...], NT).astype(BF)
+        for i in range(n // SM):
+            dt_copy(c * (n // SM) + i).wait_recv()
+        u = tn[where, :].astype(F32) * inv[where, 2:3]
+        gt = wide[where, :] + rt[where, :].astype(F32)
+        iun[b, inside, :] = project(gt, u, inv[where, 2:3]).astype(BF)
 
     loop(2, finish)
 
-    def add_x(yy):
-        v = rc_lo[yy * 4 + x].astype(F32)
+    def fold(rc, mine, recv, out):
+        v = rc[mine].astype(F32)
         for d in range(3):
-            v = v + rx[d, yy].astype(F32)
-        ba[yy] = v.astype(BF)
-
-    def add_y(xx):
-        v = rc_hi[y * 4 + xx].astype(F32)
-        for d in range(3):
-            v = v + ry[d, xx].astype(F32)
-        bb[xx] = v.astype(BF)
+            v = v + recv[d].astype(F32)
+        zero = jnp.zeros((HP - HR, v.shape[1]), F32)
+        for i in range(4):
+            out[i] = jnp.concatenate([v[i * HR : (i + 1) * HR, :], zero], axis=0).astype(BF)
 
     for copy in xc:
         copy.wait()
-    loop(4, add_x)
+    fold(rc_lo, x, rx, ba)
     second = [remote(ba.at[ys[d]], r2a.at[d], y2_send.at[d], y2_recv.at[d], y_devs[d]) for d in range(3)]
     for copy in second:
         copy.start()
     for copy in yc:
         copy.wait()
-    loop(4, add_y)
+    fold(rc_hi, y, ry, bb)
     third = [remote(bb.at[xs[d]], r2b.at[d], x2_send.at[d], x2_recv.at[d], x_devs[d]) for d in range(3)]
     for copy in third:
         copy.start()
@@ -408,13 +426,16 @@
     zs[0, :, pl.ds(LO, HI)] = hi.astype(BF)
     z0 = remote(zs.at[0], zr.at[0], z_send.at[0], z_recv.at[0], p_dev)
     z0.start()
+    di_copy(NSM - 1).start()
     z0.wait()
     zs[1] = (zs[0].astype(F32) + zr[0].astype(F32)).astype(BF)
     z1 = remote(zs.at[1], zr.at[1], z_send.at[1], z_recv.at[1], q_dev)
     z1.start()
-    loop(4, finish, 3)
+    dt_copy(NSM - 1).start()
+    loop(NSM - 1, lambda c: finish(c, SM), NSM - 2)
+    loop(NSM, lambda c: finish(c, SM), NSM - 1)
     l_copy.wait()
-    row_form(loss_n, ls)
+    row_form(3, ls)
     loss_out[...] = (ls[...] + lr[...]) * (1.0 / BLK)
     z1.wait()
     head_out[...] = (zs[1].astype(F32) + zr[1].astype(F32))[0:HR, :]
@@ -422,35 +443,20 @@
     def sent(c):
         f_copy(c).wait_send()
         t_copy(c).wait_send()
-
-    loop(NSM, sent)
-
-    def drain(c):
         di_copy(c).wait_send()
         dt_copy(c).wait_send()
-        pltpu.make_async_copy(iup.at[c // 2, half(c)], pooled_out.at[rows(c)], out_sem.at[0, c]).wait()
-        pltpu.make_async_copy(iun.at[c // 2, half(c)], text_out.at[rows(c)], out_sem.at[1, c]).wait()
-
-    loop(NCH, drain)
-
-
-def emit(loss, pooled, text, grad, loss_out, pooled_out, text_out, grad_out, stage, small, sem_in, sem_out):
-    reads, writes = [], []
-    for c in range(NCH):
-        for i, (src, dst) in enumerate(((pooled, pooled_out), (text, text_out))):
-            where = pl.ds(c * CH, CH)
-            reads.append(pltpu.make_async_copy(src.at[where], stage.at[i, where], sem_in.at[i, c]))
-            writes.append(pltpu.make_async_copy(stage.at[i, where], dst.at[where], sem_out.at[i, c]))
-    reads.append(pltpu.make_async_copy(grad, small, sem_in.at[2, 0]))
-    writes.append(pltpu.make_async_copy(small, grad_out, sem_out.at[2, 0]))
-    for copy in reads:
+
+    loop(NSM, sent)
+
+
+def emit(loss, pooled, text, grad, loss_out, pooled_out, text_out, grad_out, sem):
+    pairs = ((pooled, pooled_out), (text, text_out), (grad, grad_out))
+    copies = [pltpu.make_async_copy(a, b, sem.at[i]) for i, (a, b) in enumerate(pairs)]
+    for copy in copies:
         copy.start()
     for i in range(8):
         loss_out[pl.ds(i * 128, 128)] = loss[i, :]
-    for read, write in zip(reads, writes):
-        read.wait()
-        write.start()
-    for copy in writes:
+    for copy in copies:
         copy.wait()
 
 
@@ -463,48 +469,44 @@
     dma = pltpu.SemaphoreType.DMA
     loss, pooled, text, grad = pl.pallas_call(
         kernel,
-        out_shape=(
-            jax.ShapeDtypeStruct((8, 128), F32),
-            jax.ShapeDtypeStruct((ROWS, D), BF),
-            jax.ShapeDtypeStruct((ROWS, D), BF),
-            jax.ShapeDtypeStruct((HR, D), F32),
-        ),
+        out_shape=(pltpu.VMEM((8, 128), F32), blocks, blocks, pltpu.VMEM((HR, D), F32)),
         in_specs=[hbm] * 3 + [smem] * 5,
-        out_specs=(vmem, hbm, hbm, vmem),
+        out_specs=(vmem, vmem, vmem, vmem),
         scratch_shapes=[
-            big, big, big, blocks, blocks, pltpu.VMEM((D, D), BF), blocks, blocks,
+            big, big, big, blocks, blocks, pltpu.VMEM((D, D), BF),
             pltpu.VMEM((ROWS, D), F32), pltpu.VMEM((ROWS, D), F32), pltpu.VMEM((D, D), F32),
-            big, big, big, big, pltpu.VMEM((10, BLK, BLK), BF), big,
-            pltpu.VMEM((16, 2, HP, LO), BF), pltpu.VMEM((16, 2, HP, HI), BF),
-            pltpu.VMEM((16, HP, LO), BF), pltpu.VMEM((16, HP, HI), BF),
-            pltpu.VMEM((3, 4, HP, LO), BF), pltpu.VMEM((3, 4, HP, HI), BF),
+            big, big, big, big, pltpu.VMEM((12, BLK, BLK), BF), big,
+            pltpu.VMEM((2, 4, 4 * HR, LO), BF), pltpu.VMEM((2, 4, 4 * HR, HI), BF),
+            pltpu.VMEM((4, 4 * HR, LO), BF), pltpu.VMEM((4, 4 * HR, HI), BF),
+            pltpu.VMEM((3, 4 * HR, LO), BF), pltpu.VMEM((3, 4 * HR, HI), BF),
             pltpu.VMEM((4, HP, LO), BF), pltpu.VMEM((4, HP, HI), BF),
             pltpu.VMEM((3, HP, LO), BF), pltpu.VMEM((3, HP, HI), BF),
             pltpu.VMEM((2, HP, D), BF), pltpu.VMEM((2, HP, D), BF),
-            pltpu.VMEM((ROWS, 3), F32), pltpu.VMEM((2, BLK, 1), F32), pltpu.VMEM((2, BLK, 1), F32),
+            pltpu.VMEM((ROWS, 5), F32),
             pltpu.VMEM((8, 128), F32), pltpu.VMEM((8, 128), F32),
-            dma((NSM,)), dma((NSM,)), dma((NSM,)), dma((NSM,)), dma((NCH,)), dma((NCH,)), dma((NCH,)), dma((NCH,)),
-            dma((2,)), dma((4,)), dma((3, 4)), dma((3, 4)), dma((3,)), dma((3,)), dma((3,)), dma((3,)), dma((3,)), dma((3,)),
-            dma((2,)), dma((2,)), dma((3,)), dma((2, NCH)),
+            dma((NSM,)), dma((NSM,)), dma((NSM,)), dma((NSM,)), dma((NSM,)), dma((NSM,)), dma((NSM,)), dma((NSM,)),
+            dma((2,)), dma((4,)), dma((3,)), dma((3,)), dma((3,)), dma((3,)), dma((3,)), dma((3,)), dma((3,)), dma((3,)),
+            dma((2,)), dma((2,)), dma((3,)),
         ],
         compiler_params=pltpu.CompilerParams(
-            collective_id=0, has_side_effects=True, vmem_limit_bytes=63 << 20
+            collective_id=0, has_side_effects=True, vmem_limit_bytes=57 << 20
         ),
         cost_estimate=pl.CostEstimate(flops=34_000_000_000, bytes_accessed=20_000_000, transcendentals=6_000_000),
     )(features, captions, head, scaling, offset, jnp.swapaxes(img, 2, 3), jnp.swapaxes(cap, 2, 3), cnt)
-    return pl.pallas_call(
+    loss, pooled, text, grad = pl.pallas_call(
         emit,
         out_shape=(
             jax.ShapeDtypeStruct((ROWS,), F32),
-            jax.ShapeDtypeStruct((ROWS, D), BF),
-            jax.ShapeDtypeStruct((ROWS, D), BF),
+            jax.ShapeDtypeStruct((2, BLK, D), BF),
+            jax.ShapeDtypeStruct((2, BLK, D), BF),
             jax.ShapeDtypeStruct((HR, D), F32),
         ),
         in_specs=[vmem, hbm, hbm, hbm],
         out_specs=(vmem, hbm, hbm, hbm),
-        scratch_shapes=[pltpu.VMEM((2, ROWS, D), BF), pltpu.VMEM((HR, D), F32), dma((3, NCH)), dma((3, NCH))],
-        compiler_params=pltpu.CompilerParams(vmem_limit_bytes=63 << 20),
-    )(loss, pooled, text, grad)
+        scratch_shapes=[dma((3,))],
+        compiler_params=pltpu.CompilerParams(vmem_limit_bytes=4 << 20),
+    )(*(pltpu.with_memory_space_constraint(v, pltpu.VMEM) for v in (loss, pooled, text, grad)))
+    return loss, pooled.reshape(ROWS, D), text.reshape(ROWS, D), grad
 
 
 def solution(mesh):

time: 133 us -> 126 us (0.947)
  Pallas kernels: 130 us -> 123 us
    pallas_call x1, Pallas kernels: 124 us -> 120 us  [per_device(): pl.pallas_call(kernel, out_shape=(pltpu.VMEM((8, 128), F32), blocks, bloc...]
    pallas_call x1, Pallas kernels: 5.51 us -> 2.85 us  [per_device(): pl.pallas_call(emit, out_shape=(jax.ShapeDtypeStruct((ROWS,), F32), jax.S...]
where the time goes in v3:
time: 126 us; the launch traced here: 125 us
  Pallas kernels  123 us (98%)
  between operations  2.11 us (2%)
    pallas_call x1, Pallas kernels, per_device(): pl.pallas_call(kernel, out_shape=(pltpu.VMEM((8, 128), F32), blocks, bloc...  120 us
    pallas_call x1, Pallas kernels, per_device(): pl.pallas_call(emit, out_shape=(jax.ShapeDtypeStruct((ROWS,), F32), jax.S...  2.85 us

profile of v3, /device:TPU:0, one launch (start us, length us, event | category | flops | bytes accessed | tf_op | source)
XLA Modules:
  0.0 125.0 jit_solution(10463510628137523771)
XLA Ops:
  1.9 120.1 %shard_map.111 = (f32[8,128]{1,0:T(8,128)S(1)}, bf16[2,512,1152]{2,1,0:T(8,128)(2,1)S(1)}, bf16[2,512,1152]{2,1,0:T(8,128)(2,1)S(1)}, f32[36,1152]{1,0:T(8,128)S(1)}) custom-call(bf16[1024,1152]{1,0:T(8,128)(2,1)} %f_hbm.1, bf16[1024,1152]{1,0:T(8,128)(2,1)} %t_hbm.1, bf16[1152,1152]{1,0:T(8,128)(2,1)} %w_hbm.1, f32[1]{0:T(128)S(6)} %copy.12.scale_ref, ...), custom_call_target="tpu_custom_call" | custom-call | flops 33999998976 | bytes 20000000 | tf_op jit(solution)/shard_map/pallas_call | solution.py:470
  122.0 2.8 %shard_map.112 = (f32[1024]{0:T(1024)}, bf16[2,512,1152]{2,1,0:T(8,128)(2,1)}, bf16[2,512,1152]{2,1,0:T(8,128)(2,1)}, f32[36,1152]{1,0:T(8,128)}) custom-call(f32[8,128]{1,0:T(8,128)S(1)} %get-tuple-element.12.loss, bf16[2,512,1152]{2,1,0:T(8,128)(2,1)S(1)} %get-tuple-element.13.pooled, bf16[2,512,1152]{2,1,0:T(8,128)(2,1)S(1)} %get-tuple-element.14.text, ...), custom_call_target="tpu_custom_call" | custom-call | tf_op jit(solution)/shard_map/pallas_call | solution.py:496

commit v4 on v3

--- a/solution.py
+++ b/solution.py
@@ -18,7 +18,7 @@
 EPS = 1e-06
 HR = 36
 HP = 48
-LO = 512
+LO = 640
 HI = D - LO
 BF = jnp.bfloat16
 F32 = jnp.float32
@@ -33,8 +33,9 @@
 
 
 def kernel(
-    f_hbm, t_hbm, w_hbm, scale_ref, offset_ref, img_ref, cap_ref, cnt_ref,
+    f_hbm, t_hbm, w_hbm, scale_ref, offset_ref, img_hbm, cap_hbm, cnt_hbm,
     loss_out, iup, iun, head_out,
+    img_ref, cap_ref, cnt_ref,
     fn, fp, tn, tun, tq, w, unit32, din, wide, si, st, ri, rt, gs, ep,
     hs_lo, hs_hi, rc_lo, rc_hi, rx, ry, ba, bb, r2a, r2b, zs, zr, inv, ls, lr,
     f_send, f_recv, t_send, t_recv, di_send, di_recv, dt_send, dt_recv,
@@ -65,6 +66,12 @@
             src_ref=src, dst_ref=dst, send_sem=send, recv_sem=recv, device_id=dev, device_id_type=MESH
         )
 
+    scalars = [
+        pltpu.make_async_copy(src, dst, in_sem.at[3 + i])
+        for i, (src, dst) in enumerate(((img_hbm, img_ref), (cap_hbm, cap_ref), (cnt_hbm, cnt_ref)))
+    ]
+    for copy in scalars:
+        copy.start()
     barrier = pltpu.get_barrier_semaphore()
     peers = [p_dev, q_dev, c_dev] + x_devs + y_devs
     for dev in peers:
@@ -105,6 +112,8 @@
     f_in.start()
     t_in.start()
 
+    for copy in scalars:
+        copy.wait()
     scale = scale_ref[0]
     offset = offset_ref[0]
 
@@ -277,14 +286,13 @@
     piece(0, 0, 512, 1, 384, 128)
     piece(1, 0, 384, 1, 384, 128)
 
-    def send_text(c, last=False):
+    def send_text(c):
         k = c // 2
         sel_b = jnp.where(k == 0, pair_b[0][0], pair_b[1][0])
         sel_c = jnp.where(k == 0, pair_c[0][0], pair_c[1][0])
         st[rows(c), :] = back_text(c, ((6 + k, iun, sel_b), (8 + 2 * k + sel_c, iup, sel_c))).astype(BF)
         dt_copy(2 * c).start()
-        if not last:
-            dt_copy(2 * c + 1).start()
+        dt_copy(2 * c + 1).start()
 
     def send_image(c, last=False):
         b = c // 2
@@ -347,8 +355,6 @@
     head(hi_cols, hs_hi, True)
     c_hi = remote(hs_hi.at[1 - core], rc_hi, c_sem.at[2], c_sem.at[3], c_dev)
     c_hi.start()
-    loop(NCH - 1, send_text, 2)
-    loop(NCH, lambda c: send_text(c, True), NCH - 1)
 
     def add_core(rc, hs):
         def step(j):
@@ -361,6 +367,7 @@
     xc = [remote(rc_lo.at[xs[d]], rx.at[d], x_send.at[d], x_recv.at[d], x_devs[d]) for d in range(3)]
     for copy in xc:
         copy.start()
+    loop(NCH, send_text, 2)
     c_hi.wait()
     add_core(rc_hi, hs_hi)
     yc = [
@@ -431,7 +438,6 @@
     zs[1] = (zs[0].astype(F32) + zr[0].astype(F32)).astype(BF)
     z1 = remote(zs.at[1], zr.at[1], z_send.at[1], z_recv.at[1], q_dev)
     z1.start()
-    dt_copy(NSM - 1).start()
     loop(NSM - 1, lambda c: finish(c, SM), NSM - 2)
     loop(NSM, lambda c: finish(c, SM), NSM - 1)
     l_copy.wait()
@@ -450,8 +456,11 @@
 
 
 def emit(loss, pooled, text, grad, loss_out, pooled_out, text_out, grad_out, sem):
-    pairs = ((pooled, pooled_out), (text, text_out), (grad, grad_out))
-    copies = [pltpu.make_async_copy(a, b, sem.at[i]) for i, (a, b) in enumerate(pairs)]
+    copies = [pltpu.make_async_copy(grad, grad_out, sem.at[8])]
+    for i in range(4):
+        where = pl.ds(i % 2 * CH, CH)
+        copies.append(pltpu.make_async_copy(pooled.at[i // 2, where], pooled_out.at[i // 2, where], sem.at[i]))
+        copies.append(pltpu.make_async_copy(text.at[i // 2, where], text_out.at[i // 2, where], sem.at[4 + i]))
     for copy in copies:
         copy.start()
     for i in range(8):
@@ -470,9 +479,10 @@
     loss, pooled, text, grad = pl.pallas_call(
         kernel,
         out_shape=(pltpu.VMEM((8, 128), F32), blocks, blocks, pltpu.VMEM((HR, D), F32)),
-        in_specs=[hbm] * 3 + [smem] * 5,
+        in_specs=[hbm] * 3 + [smem] * 2 + [hbm] * 3,
         out_specs=(vmem, vmem, vmem, vmem),
         scratch_shapes=[
+            pltpu.SMEM((4, 1, 2, 4), jnp.int32), pltpu.SMEM((4, 1, 2, 4), jnp.int32), pltpu.SMEM((4, 1, 4), jnp.int32),
             big, big, big, blocks, blocks, pltpu.VMEM((D, D), BF),
             pltpu.VMEM((ROWS, D), F32), pltpu.VMEM((ROWS, D), F32), pltpu.VMEM((D, D), F32),
             big, big, big, big, pltpu.VMEM((12, BLK, BLK), BF), big,
@@ -486,7 +496,7 @@
             pltpu.VMEM((8, 128), F32), pltpu.VMEM((8, 128), F32),
             dma((NSM,)), dma((NSM,)), dma((NSM,)), dma((NSM,)), dma((NSM,)), dma((NSM,)), dma((NSM,)), dma((NSM,)),
             dma((2,)), dma((4,)), dma((3,)), dma((3,)), dma((3,)), dma((3,)), dma((3,)), dma((3,)), dma((3,)), dma((3,)),
-            dma((2,)), dma((2,)), dma((3,)),
+            dma((2,)), dma((2,)), dma((6,)),
         ],
         compiler_params=pltpu.CompilerParams(
             collective_id=0, has_side_effects=True, vmem_limit_bytes=57 << 20
@@ -503,7 +513,7 @@
         ),
         in_specs=[vmem, hbm, hbm, hbm],
         out_specs=(vmem, hbm, hbm, hbm),
-        scratch_shapes=[dma((3,))],
+        scratch_shapes=[dma((9,))],
         compiler_params=pltpu.CompilerParams(vmem_limit_bytes=4 << 20),
     )(*(pltpu.with_memory_space_constraint(v, pltpu.VMEM) for v in (loss, pooled, text, grad)))
     return loss, pooled.reshape(ROWS, D), text.reshape(ROWS, D), grad

time: 126 us -> 124 us (0.984)
  no operation moved by 1% of the time
where the time goes in v4:
time: 124 us
  Pallas kernels  122 us (98%)
  between operations  2.11 us (2%)
    pallas_call x1, Pallas kernels, per_device(): pl.pallas_call(kernel, out_shape=(pltpu.VMEM((8, 128), F32), blocks, bloc...  119 us
    pallas_call x1, Pallas kernels, per_device(): pl.pallas_call(emit, out_shape=(jax.ShapeDtypeStruct((ROWS,), F32), jax.S...  2.9 us

profile of v4, /device:TPU:0, one launch (start us, length us, event | category | flops | bytes accessed | tf_op | source)
XLA Modules:
  0.0 123.9 jit_solution(9456857968840976363)
XLA Ops:
  1.9 118.9 %shard_map.111 = (f32[8,128]{1,0:T(8,128)S(1)}, bf16[2,512,1152]{2,1,0:T(8,128)(2,1)S(1)}, bf16[2,512,1152]{2,1,0:T(8,128)(2,1)S(1)}, f32[36,1152]{1,0:T(8,128)S(1)}) custom-call(bf16[1024,1152]{1,0:T(8,128)(2,1)} %f_hbm.1, bf16[1024,1152]{1,0:T(8,128)(2,1)} %t_hbm.1, bf16[1152,1152]{1,0:T(8,128)(2,1)} %w_hbm.1, f32[1]{0:T(128)S(6)} %copy.12.scale_ref, ...), custom_call_target="tpu_custom_call" | custom-call | flops 33999998976 | bytes 20000000 | tf_op jit(solution)/shard_map/pallas_call | solution.py:479
  120.8 2.9 %shard_map.112 = (f32[1024]{0:T(1024)}, bf16[2,512,1152]{2,1,0:T(8,128)(2,1)}, bf16[2,512,1152]{2,1,0:T(8,128)(2,1)}, f32[36,1152]{1,0:T(8,128)}) custom-call(f32[8,128]{1,0:T(8,128)S(1)} %get-tuple-element.12.loss, bf16[2,512,1152]{2,1,0:T(8,128)(2,1)S(1)} %get-tuple-element.13.pooled, bf16[2,512,1152]{2,1,0:T(8,128)(2,1)S(1)} %get-tuple-element.14.text, ...), custom_call_target="tpu_custom_call" | custom-call | tf_op jit(solution)/shard_map/pallas_call | solution.py:506

commit v5 on v4

--- a/solution.py
+++ b/solution.py
@@ -90,6 +90,12 @@
     def part(c):
         return pl.ds(pl.multiple_of(lax.rem(c, 4) * SM, SM), SM)
 
+    def span(c, n):
+        return pl.ds(pl.multiple_of(c * n, SM), n)
+
+    def inside(c, n):
+        return pl.ds(pl.multiple_of(lax.rem(c, BLK // n) * n, SM), n)
+
     def f_copy(c):
         return remote(f_hbm.at[small(c)], fp.at[small(c)], f_send.at[c], f_recv.at[c], p_dev)
 
@@ -222,43 +228,49 @@
 
     loop(NCH, own_diag)
 
-    def arrive(c):
-        b = c // 4
+    def arrive_image(c):
         f_copy(c).wait_recv()
         unit, r = embed(fp, small(c))
         wide[small(c), :] = unit
         inv[small(c), 1:2] = r
-        u = unit.astype(BF)
-        iup[b, part(c), :] = u
-        total = None
+        inv[small(c), 4:5] = jnp.zeros((SM, 1), F32)
+        iup[c // 4, part(c), :] = unit.astype(BF)
+
+    def near(c):
+        b = c // 4
+        total = inv[small(c), 4:5]
         for k in range(2):
             sel, live = pair_a[k]
             keep = live * hit(sel, b)
-            e = jnp.exp(mm(u, tun[k], NT) * scale + offset)
+            e = jnp.exp(mm(iup[b, part(c), :], tun[k], NT) * scale + offset)
             gs[2 + 2 * k + b, part(c), :] = (e / (1.0 + e) * keep).astype(BF)
-            v = jnp.sum(jnp.log1p(e), axis=1, keepdims=True) * keep
-            total = v if total is None else total + v
+            total = total + jnp.sum(jnp.log1p(e), axis=1, keepdims=True) * keep
         inv[small(c), 4:5] = total
+
+    def arrive_text(c):
         t_copy(c).wait_recv()
-        v = tq[b, part(c), :].astype(F32)
-        tq[b, part(c), :] = (v * norm(v)).astype(BF)
+        v = tq[c // 4, part(c), :].astype(F32)
+        tq[c // 4, part(c), :] = (v * norm(v)).astype(BF)
+
+    def arrive(c):
+        arrive_image(c)
+        near(c)
+        arrive_text(c)
 
     loop(4, arrive)
     tile_own(0, 6)
 
-    def back_text(c, parts):
-        cols = half(c)
+    def back_text(cols, parts):
         out = None
         for slot, images, sel in parts:
             v = mm(gs[slot, :, cols], images[sel], TN)
             out = v if out is None else out + v
         return out * scale
 
-    def back_image(c, parts):
-        b = c // 2
+    def back_image(b, lines, parts):
         out = None
         for slot, texts, k, sel in parts:
-            g = gs[slot, half(c), :]
+            g = gs[slot, lines, :]
             if sel is not None:
                 g = (g.astype(F32) * hit(sel, b)).astype(BF)
             v = mm(g, texts[k], NN)
@@ -266,7 +278,7 @@
         return out * scale
 
     def own_first(c):
-        din[rows(c), :] = din[rows(c), :] + back_image(c, ((6, tq, 0, pair_b[0][0]),))
+        din[rows(c), :] = din[rows(c), :] + back_image(c // 2, half(c), ((6, tq, 0, pair_b[0][0]),))
 
     loop(NCH, own_first)
     piece(0, 0, 256, 0, 0, 512)
@@ -280,36 +292,36 @@
     piece(1, 256, 128, 1, 0, 384)
     piece(0, 0, 512, 1, 256, 128)
     piece(1, 0, 256, 1, 256, 128)
-    loop(NSM, arrive, 7)
-    piece(1, 384, 128, 0, 0, 512)
-    piece(1, 384, 128, 1, 0, 512)
-    piece(0, 0, 512, 1, 384, 128)
-    piece(1, 0, 384, 1, 384, 128)
-
-    def send_text(c):
-        k = c // 2
+    def send_text(c, n=CH):
+        k = c // (BLK // n)
         sel_b = jnp.where(k == 0, pair_b[0][0], pair_b[1][0])
         sel_c = jnp.where(k == 0, pair_c[0][0], pair_c[1][0])
-        st[rows(c), :] = back_text(c, ((6 + k, iun, sel_b), (8 + 2 * k + sel_c, iup, sel_c))).astype(BF)
-        dt_copy(2 * c).start()
-        dt_copy(2 * c + 1).start()
-
-    def send_image(c, last=False):
-        b = c // 2
+        v = back_text(inside(c, n), ((6 + k, iun, sel_b), (8 + 2 * k + sel_c, iup, sel_c)))
+        st[span(c, n), :] = v.astype(BF)
+        for i in range(n // SM):
+            dt_copy(c * (n // SM) + i).start()
+
+    def send_image(c, n=CH, held=0):
+        b = c // (BLK // n)
         g = back_image(
-            c,
-            ((2 + b, tun, 0, None), (4 + b, tun, 1, None), (8 + b, tq, 0, None), (10 + b, tq, 1, None)),
+            b, inside(c, n), ((2 + b, tun, 0, None), (4 + b, tun, 1, None), (8 + b, tq, 0, None), (10 + b, tq, 1, None))
         )
-        si[rows(c), :] = g.astype(BF)
-        di_copy(2 * c).start()
-        if not last:
-            di_copy(2 * c + 1).start()
-        ep[rows(c), :] = project(g, wide[rows(c), :], inv[rows(c), 1:2]).astype(BF)
-
-    loop(1, send_image)
-    loop(1, send_text)
+        si[span(c, n), :] = g.astype(BF)
+        for i in range(n // SM - held):
+            di_copy(c * (n // SM) + i).start()
+        ep[span(c, n), :] = project(g, wide[span(c, n), :], inv[span(c, n), 1:2]).astype(BF)
+
+    loop(NSM, arrive_text, NSM - 1)
+    piece(0, 0, 512, 1, 384, 128)
+    loop(2, lambda c: send_image(c, SM))
+    loop(NSM, arrive_image, NSM - 1)
+    piece(1, 384, 128, 0, 0, 512)
+    loop(2, lambda c: send_text(c, SM))
+    loop(NSM, near, NSM - 1)
+    piece(1, 384, 128, 1, 0, 512)
+    piece(1, 0, 384, 1, 384, 128)
     loop(NCH - 1, send_image, 1)
-    loop(NCH, lambda c: send_image(c, True), NCH - 1)
+    loop(NCH, lambda c: send_image(c, CH, 1), NCH - 1)
     loop(2, send_text, 1)
 
     def row_form(at_col, out):
@@ -323,7 +335,7 @@
     tile_own(1, 7)
 
     def own_image(c):
-        g = din[rows(c), :] + back_image(c, ((7, tq, 1, pair_b[1][0]),))
+        g = din[rows(c), :] + back_image(c // 2, half(c), ((7, tq, 1, pair_b[1][0]),))
         din[rows(c), :] = g
         tun[c // 2, half(c), :] = project(g, unit32[rows(c), :], inv[rows(c), 0:1]).astype(BF)
 
@@ -385,19 +397,18 @@
     loop(NCH, own_text)
 
     def finish(c, n=CH):
-        where = pl.ds(pl.multiple_of(c * n, SM), n)
-        inside = pl.ds(pl.multiple_of(lax.rem(c, BLK // n) * n, SM), n)
+        where = span(c, n)
         b = c // (BLK // n)
         for i in range(n // SM):
             di_copy(c * (n // SM) + i).wait_recv()
         g = din[where, :] + ri[where, :].astype(F32)
         eg = project(g, unit32[where, :], inv[where, 0:1]).astype(BF)
-        iup[b, inside, :] = mm(eg, w[...], NT).astype(BF)
+        iup[b, inside(c, n), :] = mm(eg, w[...], NT).astype(BF)
         for i in range(n // SM):
             dt_copy(c * (n // SM) + i).wait_recv()
         u = tn[where, :].astype(F32) * inv[where, 2:3]
         gt = wide[where, :] + rt[where, :].astype(F32)
-        iun[b, inside, :] = project(gt, u, inv[where, 2:3]).astype(BF)
+        iun[b, inside(c, n), :] = project(gt, u, inv[where, 2:3]).astype(BF)
 
     loop(2, finish)
 

time: 124 us -> 122 us (0.984)
  Pallas kernels: 122 us -> 119 us
    pallas_call x1, Pallas kernels: 119 us -> 116 us  [per_device(): pl.pallas_call(kernel, out_shape=(pltpu.VMEM((8, 128), F32), blocks, bloc...]
where the time goes in v5:
time: 122 us
  Pallas kernels  119 us (98%)
  between operations  2.11 us (2%)
    pallas_call x1, Pallas kernels, per_device(): pl.pallas_call(kernel, out_shape=(pltpu.VMEM((8, 128), F32), blocks, bloc...  116 us
    pallas_call x1, Pallas kernels, per_device(): pl.pallas_call(emit, out_shape=(jax.ShapeDtypeStruct((ROWS,), F32), jax.S...  2.9 us

profile of v5, /device:TPU:0, one launch (start us, length us, event | category | flops | bytes accessed | tf_op | source)
XLA Modules:
  0.0 121.5 jit_solution(12718399910774120104)
XLA Ops:
  1.9 116.5 %shard_map.111 = (f32[8,128]{1,0:T(8,128)S(1)}, bf16[2,512,1152]{2,1,0:T(8,128)(2,1)S(1)}, bf16[2,512,1152]{2,1,0:T(8,128)(2,1)S(1)}, f32[36,1152]{1,0:T(8,128)S(1)}) custom-call(bf16[1024,1152]{1,0:T(8,128)(2,1)} %f_hbm.1, bf16[1024,1152]{1,0:T(8,128)(2,1)} %t_hbm.1, bf16[1152,1152]{1,0:T(8,128)(2,1)} %w_hbm.1, f32[1]{0:T(128)S(6)} %copy.12.scale_ref, ...), custom_call_target="tpu_custom_call" | custom-call | flops 33999998976 | bytes 20000000 | tf_op jit(solution)/shard_map/pallas_call | solution.py:490
  118.4 2.9 %shard_map.112 = (f32[1024]{0:T(1024)}, bf16[2,512,1152]{2,1,0:T(8,128)(2,1)}, bf16[2,512,1152]{2,1,0:T(8,128)(2,1)}, f32[36,1152]{1,0:T(8,128)}) custom-call(f32[8,128]{1,0:T(8,128)S(1)} %get-tuple-element.12.loss, bf16[2,512,1152]{2,1,0:T(8,128)(2,1)S(1)} %get-tuple-element.13.pooled, bf16[2,512,1152]{2,1,0:T(8,128)(2,1)S(1)} %get-tuple-element.14.text, ...), custom_call_target="tpu_custom_call" | custom-call | tf_op jit(solution)/shard_map/pallas_call | solution.py:517

commit v6 on v5

--- a/solution.py
+++ b/solution.py
@@ -37,7 +37,7 @@
     loss_out, iup, iun, head_out,
     img_ref, cap_ref, cnt_ref,
     fn, fp, tn, tun, tq, w, unit32, din, wide, si, st, ri, rt, gs, ep,
-    hs_lo, hs_hi, rc_lo, rc_hi, rx, ry, ba, bb, r2a, r2b, zs, zr, inv, ls, lr,
+    hs_lo, hs_hi, rc_lo, rc_hi, rx, ry, ba, bb, r2a, r2b, zs, zr, zt, zu, pre, inv, ls, lr,
     f_send, f_recv, t_send, t_recv, di_send, di_recv, dt_send, dt_recv,
     l_sem, c_sem, x_send, x_recv, y_send, y_recv, x2_send, x2_recv, y2_send, y2_recv,
     z_send, z_recv, in_sem,
@@ -311,12 +311,23 @@
             di_copy(c * (n // SM) + i).start()
         ep[span(c, n), :] = project(g, wide[span(c, n), :], inv[span(c, n), 1:2]).astype(BF)
 
+    start = back_image(0, pl.ds(0, SM), ((2, tun, 0, None), (4, tun, 1, None), (8, tq, 0, None)))
+    pre[0] = start + mm(gs[10, 0:SM, 0:384], tq[1, 0:384, :], NN) * scale
+    pre[1] = back_text(pl.ds(0, SM), ((6, iun, pair_b[0][0]),))
     loop(NSM, arrive_text, NSM - 1)
     piece(0, 0, 512, 1, 384, 128)
-    loop(2, lambda c: send_image(c, SM))
+    first_image = pre[0] + mm(gs[10, 0:SM, 384:512], tq[1, 384:512, :], NN) * scale
+    si[0:SM, :] = first_image.astype(BF)
+    loop(1, lambda c: di_copy(c).start())
+    pre[0] = first_image
     loop(NSM, arrive_image, NSM - 1)
     piece(1, 384, 128, 0, 0, 512)
-    loop(2, lambda c: send_text(c, SM))
+    first_text = pre[1] + back_text(pl.ds(0, SM), ((8 + pair_c[0][0], iup, pair_c[0][0]),))
+    st[0:SM, :] = first_text.astype(BF)
+    loop(1, lambda c: dt_copy(c).start())
+    ep[0:SM, :] = project(pre[0], wide[0:SM, :], inv[0:SM, 1:2]).astype(BF)
+    loop(2, lambda c: send_image(c, SM), 1)
+    loop(2, lambda c: send_text(c, SM), 1)
     loop(NSM, near, NSM - 1)
     piece(1, 384, 128, 1, 0, 512)
     piece(1, 0, 384, 1, 384, 128)
@@ -440,22 +451,40 @@
     for d in range(3):
         lo = lo + r2a[d].astype(F32)
         hi = hi + r2b[d].astype(F32)
-    zs[0, :, pl.ds(0, LO)] = lo.astype(BF)
-    zs[0, :, pl.ds(LO, HI)] = hi.astype(BF)
-    z0 = remote(zs.at[0], zr.at[0], z_send.at[0], z_recv.at[0], p_dev)
-    z0.start()
+    v = jnp.concatenate([lo, hi], axis=1)
+    last = [v[32:HR, i * 384 : (i + 1) * 384] for i in range(3)] + [jnp.zeros((4, 384), F32)]
+    zs[0] = v[0:32, :].astype(BF)
+    zt[0] = jnp.concatenate(last, axis=0).astype(BF)
+
+    def z_copies(step, dev):
+        pairs = ((zs, zr), (zt, zu))
+        return [
+            remote(a.at[step], b.at[step], z_send.at[2 * step + i], z_recv.at[2 * step + i], dev)
+            for i, (a, b) in enumerate(pairs)
+        ]
+
+    z0 = z_copies(0, p_dev)
+    for copy in z0:
+        copy.start()
     di_copy(NSM - 1).start()
-    z0.wait()
+    for copy in z0:
+        copy.wait()
     zs[1] = (zs[0].astype(F32) + zr[0].astype(F32)).astype(BF)
-    z1 = remote(zs.at[1], zr.at[1], z_send.at[1], z_recv.at[1], q_dev)
-    z1.start()
+    zt[1] = (zt[0].astype(F32) + zu[0].astype(F32)).astype(BF)
+    z1 = z_copies(1, q_dev)
+    for copy in z1:
+        copy.start()
     loop(NSM - 1, lambda c: finish(c, SM), NSM - 2)
     loop(NSM, lambda c: finish(c, SM), NSM - 1)
     l_copy.wait()
     row_form(3, ls)
     loss_out[...] = (ls[...] + lr[...]) * (1.0 / BLK)
-    z1.wait()
-    head_out[...] = (zs[1].astype(F32) + zr[1].astype(F32))[0:HR, :]
+    for copy in z1:
+        copy.wait()
+    head_out[0:32, :] = zs[1].astype(F32) + zr[1].astype(F32)
+    last = zt[1].astype(F32) + zu[1].astype(F32)
+    for i in range(3):
+        head_out[32:HR, i * 384 : (i + 1) * 384] = last[4 * i : 4 * i + 4, :]
 
     def sent(c):
         f_copy(c).wait_send()
@@ -466,7 +495,7 @@
     loop(NSM, sent)
 
 
-def emit(loss, pooled, text, grad, loss_out, pooled_out, text_out, grad_out, sem):
+def emit(loss, pooled, text, grad, loss_out, pooled_out, text_out, grad_out, line, sem):
     copies = [pltpu.make_async_copy(grad, grad_out, sem.at[8])]
     for i in range(4):
         where = pl.ds(i % 2 * CH, CH)
@@ -475,7 +504,9 @@
     for copy in copies:
         copy.start()
     for i in range(8):
-        loss_out[pl.ds(i * 128, 128)] = loss[i, :]
+        line[pl.ds(i * 128, 128)] = loss[i, :]
+    copies.append(pltpu.make_async_copy(line, loss_out, sem.at[9]))
+    copies[-1].start()
     for copy in copies:
         copy.wait()
 
@@ -502,12 +533,13 @@
             pltpu.VMEM((3, 4 * HR, LO), BF), pltpu.VMEM((3, 4 * HR, HI), BF),
             pltpu.VMEM((4, HP, LO), BF), pltpu.VMEM((4, HP, HI), BF),
             pltpu.VMEM((3, HP, LO), BF), pltpu.VMEM((3, HP, HI), BF),
-            pltpu.VMEM((2, HP, D), BF), pltpu.VMEM((2, HP, D), BF),
+            pltpu.VMEM((2, 32, D), BF), pltpu.VMEM((2, 32, D), BF), pltpu.VMEM((2, 16, 384), BF), pltpu.VMEM((2, 16, 384), BF),
+            pltpu.VMEM((2, SM, D), F32),
             pltpu.VMEM((ROWS, 5), F32),
             pltpu.VMEM((8, 128), F32), pltpu.VMEM((8, 128), F32),
             dma((NSM,)), dma((NSM,)), dma((NSM,)), dma((NSM,)), dma((NSM,)), dma((NSM,)), dma((NSM,)), dma((NSM,)),
             dma((2,)), dma((4,)), dma((3,)), dma((3,)), dma((3,)), dma((3,)), dma((3,)), dma((3,)), dma((3,)), dma((3,)),
-            dma((2,)), dma((2,)), dma((6,)),
+            dma((4,)), dma((4,)), dma((6,)),
         ],
         compiler_params=pltpu.CompilerParams(
             collective_id=0, has_side_effects=True, vmem_limit_bytes=57 << 20
@@ -523,8 +555,8 @@
             jax.ShapeDtypeStruct((HR, D), F32),
         ),
         in_specs=[vmem, hbm, hbm, hbm],
-        out_specs=(vmem, hbm, hbm, hbm),
-        scratch_shapes=[dma((9,))],
+        out_specs=(hbm, hbm, hbm, hbm),
+        scratch_shapes=[pltpu.VMEM((ROWS,), F32), dma((10,))],
         compiler_params=pltpu.CompilerParams(vmem_limit_bytes=4 << 20),
     )(*(pltpu.with_memory_space_constraint(v, pltpu.VMEM) for v in (loss, pooled, text, grad)))
     return loss, pooled.reshape(ROWS, D), text.reshape(ROWS, D), grad

time: 122 us -> 120 us (0.984)
  Pallas kernels: 119 us -> 117 us
    pallas_call x1, Pallas kernels: 116 us -> 115 us  [per_device(): pl.pallas_call(kernel, out_shape=(pltpu.VMEM((8, 128), F32), blocks, bloc...]
where the time goes in v6:
time: 120 us; the launch traced here: 119 us
  Pallas kernels  117 us (98%)
  between operations  2.11 us (2%)
    pallas_call x1, Pallas kernels, per_device(): pl.pallas_call(kernel, out_shape=(pltpu.VMEM((8, 128), F32), blocks, bloc...  115 us

profile of v6, /device:TPU:0, one launch (start us, length us, event | category | flops | bytes accessed | tf_op | source)
XLA Modules:
  0.0 119.5 jit_solution(4010303217810889893)
XLA Ops:
  1.9 115.0 %shard_map.111 = (f32[8,128]{1,0:T(8,128)S(1)}, bf16[2,512,1152]{2,1,0:T(8,128)(2,1)S(1)}, bf16[2,512,1152]{2,1,0:T(8,128)(2,1)S(1)}, f32[36,1152]{1,0:T(8,128)S(1)}) custom-call(bf16[1024,1152]{1,0:T(8,128)(2,1)} %f_hbm.1, bf16[1024,1152]{1,0:T(8,128)(2,1)} %t_hbm.1, bf16[1152,1152]{1,0:T(8,128)(2,1)} %w_hbm.1, f32[1]{0:T(128)S(6)} %copy.12.scale_ref, ...), custom_call_target="tpu_custom_call" | custom-call | flops 33999998976 | bytes 20000000 | tf_op jit(solution)/shard_map/pallas_call | solution.py:521
  117.0 2.3 %shard_map.112 = (f32[1024]{0:T(1024)}, bf16[2,512,1152]{2,1,0:T(8,128)(2,1)}, bf16[2,512,1152]{2,1,0:T(8,128)(2,1)}, f32[36,1152]{1,0:T(8,128)}) custom-call(f32[8,128]{1,0:T(8,128)S(1)} %get-tuple-element.12.loss, bf16[2,512,1152]{2,1,0:T(8,128)(2,1)S(1)} %get-tuple-element.13.pooled, bf16[2,512,1152]{2,1,0:T(8,128)(2,1)S(1)} %get-tuple-element.14.text, ...), custom_call_target="tpu_custom_call" | custom-call | tf_op jit(solution)/shard_map/pallas_call | solution.py:549

commit v7 on v6

--- a/solution.py
+++ b/solution.py
@@ -411,15 +411,15 @@
         where = span(c, n)
         b = c // (BLK // n)
         for i in range(n // SM):
+            dt_copy(c * (n // SM) + i).wait_recv()
+        u = tn[where, :].astype(F32) * inv[where, 2:3]
+        gt = wide[where, :] + rt[where, :].astype(F32)
+        iun[b, inside(c, n), :] = project(gt, u, inv[where, 2:3]).astype(BF)
+        for i in range(n // SM):
             di_copy(c * (n // SM) + i).wait_recv()
         g = din[where, :] + ri[where, :].astype(F32)
         eg = project(g, unit32[where, :], inv[where, 0:1]).astype(BF)
         iup[b, inside(c, n), :] = mm(eg, w[...], NT).astype(BF)
-        for i in range(n // SM):
-            dt_copy(c * (n // SM) + i).wait_recv()
-        u = tn[where, :].astype(F32) * inv[where, 2:3]
-        gt = wide[where, :] + rt[where, :].astype(F32)
-        iun[b, inside(c, n), :] = project(gt, u, inv[where, 2:3]).astype(BF)
 
     loop(2, finish)
 
@@ -437,6 +437,11 @@
     second = [remote(ba.at[ys[d]], r2a.at[d], y2_send.at[d], y2_recv.at[d], y_devs[d]) for d in range(3)]
     for copy in second:
         copy.start()
+    def sent(c):
+        f_copy(c).wait_send()
+        t_copy(c).wait_send()
+
+    loop(NSM, sent)
     for copy in yc:
         copy.wait()
     fold(rc_hi, y, ry, bb)
@@ -474,11 +479,16 @@
     z1 = z_copies(1, q_dev)
     for copy in z1:
         copy.start()
-    loop(NSM - 1, lambda c: finish(c, SM), NSM - 2)
-    loop(NSM, lambda c: finish(c, SM), NSM - 1)
+    def returned(c):
+        di_copy(c).wait_send()
+        dt_copy(c).wait_send()
+
+    loop(NSM - 2, returned)
     l_copy.wait()
     row_form(3, ls)
     loss_out[...] = (ls[...] + lr[...]) * (1.0 / BLK)
+    loop(NSM - 1, lambda c: finish(c, SM), NSM - 2)
+    loop(NSM, lambda c: finish(c, SM), NSM - 1)
     for copy in z1:
         copy.wait()
     head_out[0:32, :] = zs[1].astype(F32) + zr[1].astype(F32)
@@ -486,13 +496,7 @@
     for i in range(3):
         head_out[32:HR, i * 384 : (i + 1) * 384] = last[4 * i : 4 * i + 4, :]
 
-    def sent(c):
-        f_copy(c).wait_send()
-        t_copy(c).wait_send()
-        di_copy(c).wait_send()
-        dt_copy(c).wait_send()
-
-    loop(NSM, sent)
+    loop(NSM, returned, NSM - 2)
 
 
 def emit(loss, pooled, text, grad, loss_out, pooled_out, text_out, grad_out, line, sem):

time: 120 us -> 119 us (level)
  no operation moved by 1% of the time
where the time goes in v7:
time: 119 us
  Pallas kernels  117 us (98%)
  between operations  2.11 us (2%)
    pallas_call x1, Pallas kernels, per_device(): pl.pallas_call(kernel, out_shape=(pltpu.VMEM((8, 128), F32), blocks, bloc...  114 us

profile of v7, /device:TPU:0, one launch (start us, length us, event | category | flops | bytes accessed | tf_op | source)
XLA Modules:
  0.0 118.8 jit_solution(11715154572380655411)
XLA Ops:
  1.9 114.4 %shard_map.111 = (f32[8,128]{1,0:T(8,128)S(1)}, bf16[2,512,1152]{2,1,0:T(8,128)(2,1)S(1)}, bf16[2,512,1152]{2,1,0:T(8,128)(2,1)S(1)}, f32[36,1152]{1,0:T(8,128)S(1)}) custom-call(bf16[1024,1152]{1,0:T(8,128)(2,1)} %f_hbm.1, bf16[1024,1152]{1,0:T(8,128)(2,1)} %t_hbm.1, bf16[1152,1152]{1,0:T(8,128)(2,1)} %w_hbm.1, f32[1]{0:T(128)S(6)} %copy.12.scale_ref, ...), custom_call_target="tpu_custom_call" | custom-call | flops 33999998976 | bytes 20000000 | tf_op jit(solution)/shard_map/pallas_call | solution.py:525
  116.3 2.3 %shard_map.112 = (f32[1024]{0:T(1024)}, bf16[2,512,1152]{2,1,0:T(8,128)(2,1)}, bf16[2,512,1152]{2,1,0:T(8,128)(2,1)}, f32[36,1152]{1,0:T(8,128)}) custom-call(f32[8,128]{1,0:T(8,128)S(1)} %get-tuple-element.12.loss, bf16[2,512,1152]{2,1,0:T(8,128)(2,1)S(1)} %get-tuple-element.13.pooled, bf16[2,512,1152]{2,1,0:T(8,128)(2,1)S(1)} %get-tuple-element.14.text, ...), custom_call_target="tpu_custom_call" | custom-call | tf_op jit(solution)/shard_map/pallas_call | solution.py:553

commit v8 on v7

--- a/solution.py
+++ b/solution.py
@@ -437,6 +437,7 @@
     second = [remote(ba.at[ys[d]], r2a.at[d], y2_send.at[d], y2_recv.at[d], y_devs[d]) for d in range(3)]
     for copy in second:
         copy.start()
+
     def sent(c):
         f_copy(c).wait_send()
         t_copy(c).wait_send()
@@ -448,7 +449,6 @@
     third = [remote(bb.at[xs[d]], r2b.at[d], x2_send.at[d], x2_recv.at[d], x_devs[d]) for d in range(3)]
     for copy in third:
         copy.start()
-    loop(3, finish, 2)
     for copy in second + third:
         copy.wait()
     lo = ba[y].astype(F32)
@@ -472,6 +472,7 @@
     for copy in z0:
         copy.start()
     di_copy(NSM - 1).start()
+    loop(3, finish, 2)
     for copy in z0:
         copy.wait()
     zs[1] = (zs[0].astype(F32) + zr[0].astype(F32)).astype(BF)

time: 119 us -> 119 us (level)
  no operation moved by 1% of the time
where the time goes in v8:
time: 119 us
  Pallas kernels  117 us (98%)
  between operations  2.11 us (2%)
    pallas_call x1, Pallas kernels, per_device(): pl.pallas_call(kernel, out_shape=(pltpu.VMEM((8, 128), F32), blocks, bloc...  114 us

profile of v8, /device:TPU:0, one launch (start us, length us, event | category | flops | bytes accessed | tf_op | source)
XLA Modules:
  0.0 118.8 jit_solution(9227769332492183252)
XLA Ops:
  1.9 114.4 %shard_map.111 = (f32[8,128]{1,0:T(8,128)S(1)}, bf16[2,512,1152]{2,1,0:T(8,128)(2,1)S(1)}, bf16[2,512,1152]{2,1,0:T(8,128)(2,1)S(1)}, f32[36,1152]{1,0:T(8,128)S(1)}) custom-call(bf16[1024,1152]{1,0:T(8,128)(2,1)} %f_hbm.1, bf16[1024,1152]{1,0:T(8,128)(2,1)} %t_hbm.1, bf16[1152,1152]{1,0:T(8,128)(2,1)} %w_hbm.1, f32[1]{0:T(128)S(6)} %copy.12.scale_ref, ...), custom_call_target="tpu_custom_call" | custom-call | flops 33999998976 | bytes 20000000 | tf_op jit(solution)/shard_map/pallas_call | solution.py:526
  116.3 2.3 %shard_map.112 = (f32[1024]{0:T(1024)}, bf16[2,512,1152]{2,1,0:T(8,128)(2,1)}, bf16[2,512,1152]{2,1,0:T(8,128)(2,1)}, f32[36,1152]{1,0:T(8,128)}) custom-call(f32[8,128]{1,0:T(8,128)S(1)} %get-tuple-element.12.loss, bf16[2,512,1152]{2,1,0:T(8,128)(2,1)S(1)} %get-tuple-element.13.pooled, bf16[2,512,1152]{2,1,0:T(8,128)(2,1)S(1)} %get-tuple-element.14.text, ...), custom_call_target="tpu_custom_call" | custom-call | tf_op jit(solution)/shard_map/pallas_call | solution.py:554
